TPU v7x, 128 devices: a whole 4x4x4 slice. The times are simulated.
128 devices in a mesh: hid: 4 (over y_lo, core), tok: 32 (over y_hi, x, z).
Axes of the slice: x: 4, y: 4 (y_hi: 2, y_lo: 2; y = y_hi * 2 + y_lo), z: 4, core: 2. Of those that a mesh axis runs over, the one named last changes fastest.
Arguments:
- activations: bfloat16 [32768, 14336], P('tok', 'hid'), may hold values from -6 to 6
- dictionary: bfloat16 [14336, 1024], P('hid', 'tok'), may hold values from -0.046875 to 0.046875
- second_factor: bfloat16 [1024, 256], replicated, may hold values from -0.1875 to 0.1875
- first_codes: float32 [32, 4, 256, 1024], P('tok', 'hid'), may hold values from 0.05 to 2
- second_codes: float32 [32, 4, 256, 256], P('tok', 'hid'), may hold values from 0.05 to 2
Outputs:
- first_new: float32 [32, 4, 256, 1024], P('tok', 'hid')
- second_new: float32 [32, 4, 256, 256], P('tok', 'hid')
- direction: float32 [1024, 256], P('tok')
All inputs are finite; a program needn't handle non-finite values.
Results may differ from a plain program's by a relative error of at most 0.00057.
Values may be sent and summed in bfloat16 or wider, within the bound.
A program may use at most 128 MiB of HBM per device.

v0:
```python
import jax
import jax.numpy as jnp
from jax import lax
from jax.sharding import PartitionSpec as P

HIGH = lax.Precision.HIGHEST


def mult_update(codes, lin, gmat):
    num = jnp.maximum(lin, 0.0) + jnp.dot(codes, jnp.maximum(-gmat, 0.0), precision=HIGH)
    den = jnp.maximum(-lin, 0.0) + jnp.dot(codes, jnp.maximum(gmat, 0.0), precision=HIGH)
    return codes * jnp.sqrt(num / den)


def shards(activations, dictionary, second_factor, first_codes, second_codes):
    tok_count = lax.axis_size("tok")
    block = dictionary.shape[1]
    atoms = block * tok_count
    first_width = first_codes.shape[3]
    second_width = second_codes.shape[3]
    whole_rows = lax.all_gather(dictionary, "tok", axis=1, tiled=True)
    feat_part = jnp.dot(activations, whole_rows, preferred_element_type=jnp.float32)
    gram_part = jnp.einsum("dk,dc->kc", dictionary, whole_rows, preferred_element_type=jnp.float32)
    feats = lax.psum_scatter(feat_part, "hid", scatter_dimension=0, tiled=True).astype(jnp.bfloat16)
    collected = lax.all_gather(gram_part, "tok", axis=0, tiled=True)
    gram = lax.psum(collected, "hid")
    ffull = feats.astype(jnp.float32)
    first_flat = first_codes.reshape(-1, first_width)
    first_new = mult_update(first_flat, ffull, gram)
    proj = jnp.dot(feats, second_factor, preferred_element_type=jnp.float32)
    sfull = second_factor.astype(jnp.float32)
    inner = jnp.dot(jnp.dot(sfull.T, gram, precision=HIGH), sfull, precision=HIGH)
    second_flat = second_codes.reshape(-1, second_width)
    second_new = mult_update(second_flat, proj, inner)
    cross_part = jnp.dot(ffull.T, second_new, precision=HIGH)
    codegram_part = jnp.dot(second_new.T, second_new, precision=HIGH)
    position = lax.axis_index("tok")
    cross_all, codegram = lax.psum((cross_part, codegram_part), ("hid", "tok"))
    cross_own = lax.dynamic_slice_in_dim(cross_all, position * block, block, 0)
    gram_own = lax.dynamic_slice_in_dim(gram, position * block, block, 0)
    grad = jnp.dot(jnp.dot(gram_own, sfull, precision=HIGH), codegram, precision=HIGH) - cross_own
    squares = lax.psum(jnp.sum(grad * grad), "tok")
    direction = grad / jnp.sqrt(squares / (atoms * second_width) + 1e-06)
    return (first_new.reshape(first_codes.shape), second_new.reshape(second_codes.shape), direction)


def solution(mesh):
    in_specs = (
        P("tok", "hid"),
        P("hid", "tok"),
        P(),
        P("tok", "hid", None, None),
        P("tok", "hid", None, None),
    )
    out_specs = (P("tok", "hid", None, None), P("tok", "hid", None, None), P("tok", None))
    return jax.shard_map(shards, mesh=mesh, in_specs=in_specs, out_specs=out_specs, check_vma=False)
```

profile of v0, /device:TPU:1, one launch (start us, length us, event | category | flops | bytes accessed | tf_op | source)
XLA Modules:
  0.0 587.8 jit_solution(3423381152230137099)
XLA Ops:
  7.2 0.0 copy-start
  7.2 0.0 all-gather.3.cloned.1.call-start
  7.2 0.7 all-gather.3.cloned.1.call-update
  7.9 0.0 all-gather.5.cloned.1.call-start
  8.0 103.9 %all-gather.3.cloned.1.call-done = bf16[3584,1024]{0,1:T(8,128)(2,1)} async-done(((bf16[3584,32]{0,1:T(8,128)(2,1)}), bf16[3584,1024]{0,1:T(8,128)(2,1)}) %all-gather.3.cloned.1.call-update) | async-done | bytes 7340048 | tf_op jit(solution)/shard_map/all_gather | solution.py:21
  111.9 6.1 %fusion.54 = f32[32,1024]{1,0:T(8,128)} fusion(bf16[3584,32]{0,1:T(8,128)(2,1)} %param.6, bf16[3584,1024]{0,1:T(8,128)(2,1)} %all-gather.3.cloned.1.call-done), kind=kOutput, calls=%fused_computation.45 | convolution fusion | flops 234881024 | bytes 7700480 | tf_op jit(solution)/shard_map/dk,dc->kc/dot_general | solution.py:23
  118.0 0.0 all-gather.5.cloned.1.call-update
  118.0 0.0 reduce-scatter.2.cloned.1.call-start
  118.0 13.5 %fusion.53 = f32[1024,1024]{1,0:T(8,128)} fusion(bf16[1024,3584]{1,0:T(8,128)(2,1)} %param.5, bf16[3584,1024]{0,1:T(8,128)(2,1)} %all-gather.3.cloned.1.call-done), kind=kOutput, calls=%fused_computation.44 | convolution fusion | flops 7516192768 | bytes 18874368 | tf_op jit(solution)/shard_map/dot_general | solution.py:22
  131.6 0.0 reduce-scatter.2.cloned.1.call-update
  131.6 0.0 all-reduce.4.cloned.1.call-start
  131.7 64.5 %all-gather.5.cloned.1.call-done = f32[1024,1024]{1,0:T(8,128)} async-done(((f32[32,1024]{1,0:T(8,128)}), f32[1024,1024]{1,0:T(8,128)}) %all-gather.5.cloned.1.call-update) | async-done | bytes 4194320 | tf_op jit(solution)/shard_map/all_gather | solution.py:25
  196.2 0.0 all-reduce.4.cloned.1.call-update
  196.2 0.0 all-reduce.6.cloned.1.call-start
  196.3 46.1 %reduce-scatter.2.cloned.1.call-done = f32[256,1024]{1,0:T(8,128)} async-done(((f32[1024,1024]{1,0:T(8,128)}), f32[256,1024]{1,0:T(8,128)}) %reduce-scatter.2.cloned.1.call-update) | async-done | bytes 1048592 | tf_op jit(solution)/shard_map/reduce_scatter | solution.py:24
  242.4 1.3 convert_element_type.7
  243.7 0.3 fusion.55
  244.0 93.5 %all-reduce.4.cloned.1.call-done = f32[1024,1024]{1,0:T(8,128)} async-done(((f32[1024,1024]{1,0:T(8,128)}), f32[1024,1024]{1,0:T(8,128)}) %all-reduce.4.cloned.1.call-update) | async-done | bytes 4194320 | tf_op jit(solution)/shard_map/psum | solution.py:26
  337.5 5.6 fusion.56
  343.1 1.0 fusion.57
  344.2 0.4 fusion.35
  344.6 0.5 fusion.34
  345.1 1.3 fusion.58
  346.4 1.7 fusion.59
  348.1 0.0 all-reduce.6.cloned.1.call-update
  348.2 6.4 %fusion.10 = f32[256,1024]{1,0:T(8,128)S(1)} fusion(f32[1024,1024]{1,0:T(8,128)} %all-reduce.4.cloned.1.call-done, bf16[256,1024]{1,0:T(8,128)(2,1)S(1)} %convert_element_type.7, f32[1,1,256,1024]{3,2,1,0:T(8,128)S(1)} %copy-done.3), kind=kOutput, calls=%fused_computation.8 | convolution fusion | flops 3224109056 | bytes 6815744 | tf_op jit(solution)/shard_map/dot_general | solution.py:10
  354.6 0.4 fusion.44
  354.9 5.2 fusion.28
  360.2 136.8 %all-reduce.6.cloned.1.call-done = (f32[256,256]{1,0:T(8,128)}, f32[1024,256]{1,0:T(8,128)}) async-done(((f32[256,256]{1,0:T(8,128)}, f32[1024,256]{1,0:T(8,128)}), (f32[256,256]{1,0:T(8,128)}, f32[1024,256]{1,0:T(8,128)})) %all-reduce.6.cloned.1.call-update) | async-done | bytes 1310736 | tf_op jit(solution)/shard_map/psum | solution.py:38
  497.0 1.8 multiply_reduce_fusion
  498.8 81.1 %psum.31 = f32[]{:T(128)} all-reduce(f32[]{:T(128)} %get-tuple-element.5), channel_id=1, replica_groups=mesh['hid'=4,'tok'=32] {'tok'}, use_global_device_ids=true, to_apply=%region_5.0 | all-reduce | flops 1 | bytes 8 | tf_op jit(solution)/shard_map/psum | solution.py:42
  580.6 0.6 broadcast_divide_fusion
  (9 shorter events, 0.0 us)
Async XLA Ops:
  7.2 236.5 %copy-start = (bf16[1024,256]{1,0:T(8,128)(2,1)S(1)}, bf16[1024,256]{1,0:T(8,128)(2,1)}, u32[]{:S(2)}) copy-start(bf16[1024,256]{1,0:T(8,128)(2,1)} %param.7) | copy-start | bytes 1572868
  7.2 104.7 %all-gather.3.cloned.1.call-start = ((), (), s32[]{:S(2)}) async-start(), calls=%async_computation.1 | async-start | bytes 7569408 | tf_op jit(solution)/shard_map/all_gather | solution.py:21
  7.9 188.3 %all-gather.5.cloned.1.call-start = ((), (), s32[]{:S(2)}) async-start(), calls=%async_computation.3 | async-start | bytes 4325376 | tf_op jit(solution)/shard_map/all_gather | solution.py:25
  118.0 124.4 %reduce-scatter.2.cloned.1.call-start = ((), (), s32[]{:S(2)}) async-start(), calls=%async_computation.2 | async-start | bytes 5242880 | tf_op jit(solution)/shard_map/reduce_scatter | solution.py:24
  131.6 205.9 %all-reduce.4.cloned.1.call-start = ((), (), s32[]{:S(2)}) async-start(), calls=%async_computation.4 | async-start | bytes 8388608 | tf_op jit(solution)/shard_map/psum | solution.py:26
  196.2 300.8 %all-reduce.6.cloned.1.call-start = ((), (), s32[]{:S(2)}) async-start(), calls=%async_computation.5 | async-start | bytes 2621440 | tf_op jit(solution)/shard_map/psum | solution.py:38
  243.7 100.5 %copy-start.4 = (f32[1,1,256,256]{3,2,1,0:T(8,128)S(1)}, f32[1,1,256,256]{3,2,1,0:T(8,128)}, u32[]{:S(2)}) copy-start(f32[1,1,256,256]{3,2,1,0:T(8,128)} %param.9) | copy-start | bytes 786436
  343.1 5.0 copy-start.3
  345.1 9.5 %copy-start.2 = (f32[256,256]{1,0:T(8,128)}, f32[256,256]{1,0:T(8,128)S(1)}, u32[]{:S(2)}) copy-start(f32[256,256]{1,0:T(8,128)S(1)} %fusion.34) | copy-start | bytes 786436
  348.1 6.4 %copy-start.1 = (f32[1024,1024]{1,0:T(8,128)S(1)}, f32[1024,1024]{1,0:T(8,128)}, u32[]{:S(2)}) copy-start(f32[1024,1024]{1,0:T(8,128)} %all-reduce.4.cloned.1.call-done) | copy-start | bytes 12582916
Sparse Core Ops, SparseCore 0:
  11.1 100.7 all-gather.2
  118.1 78.0 all-gather.4
  198.6 43.7 reduce-scatter.1
  244.9 92.5 all-reduce.3
  348.3 148.7 all-reduce.5
where the time goes:
time: 600 us; the launch traced here: 588 us
  waiting for transfers between devices  446 us (74%)
  blocking collectives  81.1 us (14%)
  matrix products  44.3 us (7%)
  between operations  14.6 us (2%)
    psum x1, waiting for transfers between devices, shards(): cross_all, codegram = lax.psum((cross_part, codegram_part), ('hid', 'tok'))  137 us
    all_gather x1, waiting for transfers between devices, shards(): whole_rows = lax.all_gather(dictionary, 'tok', axis=1, tiled=True)  104 us
    psum x1, waiting for transfers between devices, shards(): gram = lax.psum(collected, 'hid')  93.5 us
    psum x1, blocking collectives, shards(): squares = lax.psum(jnp.sum(grad * grad), 'tok')  81.1 us
    all_gather x1, waiting for transfers between devices, shards(): collected = lax.all_gather(gram_part, 'tok', axis=0, tiled=True)  64.5 us
    reduce_scatter x1, waiting for transfers between devices, shards(): lax.psum_scatter(feat_part, 'hid', scatter_dimension=0, tiled=True)  46.1 us
    dot_general x1, matrix products, shards(): jnp.dot(activations, whole_rows, preferred_element_type=jnp.float32)  13.5 us
  transfers between devices with their start and end apart: 5, of which 5 were waited for; matrix products, arithmetic and copies ran while one was open for 5% of the time, Pallas kernels for 0%

commit v1 on v0

v1 whole, which is shorter than its diff:
```python
import functools

import jax
import jax.numpy as jnp
from jax import lax
from jax.experimental import pallas as pl
from jax.experimental.pallas import tpu as pltpu
from jax.sharding import PartitionSpec as P

F32 = jnp.float32
BF16 = jnp.bfloat16
MESH = pl.DeviceIdType.MESH
NN = (((1,), (0,)), ((), ()))
NT = (((1,), (1,)), ((), ()))


def dot(a, b, dims=NN):
    return lax.dot_general(a, b, dims, preferred_element_type=F32)


def split(a):
    hi = a.astype(BF16)
    return hi, (a - hi.astype(F32)).astype(BF16)


def dot3(a, b, dims=NN):
    ah, al = a
    bh, bl = b
    return dot(ah, bh, dims) + (dot(al, bh, dims) + dot(ah, bl, dims))


def pos_neg(g):
    p = split(jnp.maximum(g, 0.0))
    n = split(jnp.maximum(-g, 0.0))
    return p, n


def kernel(
    act_hbm, dt_hbm, s_hbm, h1_hbm, h2_hbm,
    first_hbm, second_hbm, dir_hbm,
    act, w, s, h1, h2,
    pl_f, pl_g, rc_f, rc_g, ys_f, ys_g, ry_f, ry_g,
    fp, gown, sp, st, perm, eye, h1h, h1l, fn, ft,
    gsb, gb, first_v, second_v,
    gp, rcgp, gs1, r1a, r1b, ab2, r2a, r2b, ab3, r3, dirh, dirf,
    nrm, nrx, nrz, nry, nrc,
    local_sem, ga_send, ga_recv, fe_send, fe_recv, gs_send, gs_recv, gg_send, gg_recv,
    rs_send, rs_recv, no_send, no_recv,
):
    hid = lax.axis_index("hid")
    tok = lax.axis_index("tok")
    yl, c = hid // 2, hid % 2
    yh, x, z = tok // 16, (tok // 4) % 4, tok % 4
    y = yh * 2 + yl
    sub = h1.shape[0]

    def dev(yl_, c_, yh_, x_, z_):
        return (yl_ * 2 + c_, yh_ * 16 + x_ * 4 + z_)

    core = dev(yl, 1 - c, yh, x, z)
    ylp = dev(1 - yl, c, yh, x, z)
    yhp = dev(yl, c, 1 - yh, x, z)

    def xdev(d):
        return dev(yl, c, yh, (x + d) % 4, z)

    def zdev(d):
        return dev(yl, c, yh, x, (z + d) % 4)

    def ydev(d):
        yy = (y + d) % 4
        return dev(yy % 2, c, yy // 2, x, z)

    acopy = pltpu.make_async_copy(act_hbm, act, local_sem.at[0])
    acopy.start()
    own_b = yh * 16 + x * 4 + z
    dcopy = pltpu.make_async_copy(dt_hbm, w.at[own_b], local_sem.at[1])
    dcopy.start()
    scopy = pltpu.make_async_copy(s_hbm, s, local_sem.at[2])
    scopy.start()
    h1copy = pltpu.make_async_copy(h1_hbm, h1, local_sem.at[3])
    h1copy.start()
    h2copy = pltpu.make_async_copy(h2_hbm, h2, local_sem.at[4])
    h2copy.start()

    barrier = pltpu.get_barrier_semaphore()
    for d in (1, 2, 3):
        for who in (xdev(d), zdev(d), ydev(d)):
            pl.semaphore_signal(barrier, inc=1, device_id=who, device_id_type=MESH)
    pl.semaphore_signal(barrier, inc=1, device_id=core, device_id_type=MESH)
    pl.semaphore_wait(barrier, 10)

    pending = []

    def send(src, dst, ss, rs, who):
        cp = pltpu.make_async_remote_copy(
            src_ref=src, dst_ref=dst, send_sem=ss, recv_sem=rs, device_id=who, device_id_type=MESH
        )
        cp.start()
        pending.append(cp)
        return cp

    def part(o):
        p = (yh + o) % 2
        u = x + p * (z - x)
        v = z + p * (x - z)
        return p, u, v

    def blk(p, u_, v_):
        return p * 16 + u_ * (4 - 3 * p) + v_ * (1 + 3 * p)

    DU = (0, 3, 1, 2)

    def gdev(o, du, dv):
        p, u, v = part(o)
        u_, v_ = (u + du) % 4, (v + dv) % 4
        return (hid, yh * 16 + u_ * (4 - 3 * p) + v_ * (1 + 3 * p))

    def gsend(o, k, b, who, rows=None, src=None):
        dst = w.at[b] if rows is None else w.at[b, pl.ds(rows, 16)]
        if src is None:
            src = dst
        return send(src, dst, ga_send.at[o, k], ga_recv.at[o, k], who)

    def gblk(o, du, dv):
        p, u, v = part(o)
        return blk(p, (u + du) % 4, (v + dv) % 4)

    gd = {}

    def start_ph1(o, src=None):
        b = gblk(o, 0, 0)
        gd[o, 0] = gsend(o, 0, b, gdev(o, 1, 0), src=src)
        gd[o, 1] = gsend(o, 1, b, gdev(o, 3, 0), src=src)

    def start_ph2(o, i, src=None):
        b = gblk(o, DU[i], 0)
        gd[o, 4 + 4 * i] = gsend(o, 4 + 4 * i, b, gdev(o, 0, 1), src=src)
        gd[o, 5 + 4 * i] = gsend(o, 5 + 4 * i, b, gdev(o, 0, 3), src=src)

    def fwd_ph1(o):
        gd[o, 0].wait_recv()
        gd[o, 2] = gsend(o, 2, gblk(o, 3, 0), gdev(o, 1, 0), rows=0)
        gd[o, 1].wait_recv()
        gd[o, 3] = gsend(o, 3, gblk(o, 1, 0), gdev(o, 3, 0), rows=16)

    def fwd_ph2(o, i):
        gd[o, 4 + 4 * i].wait_recv()
        gd[o, 6 + 4 * i] = gsend(o, 6 + 4 * i, gblk(o, DU[i], 3), gdev(o, 0, 1), rows=0)
        gd[o, 5 + 4 * i].wait_recv()
        gd[o, 7 + 4 * i] = gsend(o, 7 + 4 * i, gblk(o, DU[i], 1), gdev(o, 0, 3), rows=16)

    def end_ph1(o):
        gd[o, 2].wait_recv()
        gd[o, 3].wait_recv()

    def end_ph2(o, i):
        gd[o, 6 + 4 * i].wait_recv()
        gd[o, 7 + 4 * i].wait_recv()

    fd = {}

    def chunk_of(o, i):
        p, u, v = part(o)
        return p * 4 + (u + DU[i]) % 4

    def group(i):
        def rows_of(o):
            return jnp.concatenate([w[gblk_abs(o, i, j)] for j in range(4)], axis=0)

        def gblk_abs(o, i, j):
            p, u, v = part(o)
            return blk(p, (u + DU[i]) % 4, j)

        def weights():
            return jnp.concatenate([rows_of(0), rows_of(1)], axis=0)

        lrows = jnp.concatenate([w[x * 4 + z], w[16 + x * 4 + z]], axis=0)
        g = dot(lrows, weights(), NT)
        pl_g[i] = g.reshape(2, 32, g.shape[1])
        fd[i, 0] = send(pl_g.at[i, 1 - c], rc_g.at[i], fe_send.at[i, 0], fe_recv.at[i, 0], core)

        def body(h, carry):
            pl_f[i, h // 2, h % 2] = dot(act[pl.ds(pl.multiple_of(h * sub, sub), sub), :], weights(), NT)
            return carry

        lax.fori_loop(0, 4, body, 0)
        fd[i, 1] = send(pl_f.at[i, :, 1 - c], rc_f.at[i], fe_send.at[i, 1], fe_recv.at[i, 1], core)

    def reduce_core_g(i):
        fd[i, 0].wait_recv()
        ys_g[i] = pl_g[i, c] + rc_g[i]
        fd[i, 2] = send(ys_g.at[i], ry_g.at[i], fe_send.at[i, 2], fe_recv.at[i, 2], ylp)

    def reduce_core_f(i):
        fd[i, 1].wait_recv()
        ys_f[i] = pl_f[i, 1 - yl, c] + rc_f[i, 1 - yl]
        fd[i, 3] = send(ys_f.at[i], ry_f.at[i], fe_send.at[i, 3], fe_recv.at[i, 3], ylp)

    def lanes(q):
        return pl.ds(pl.multiple_of(q * 128, 128), 128)

    def reduce_y_g(i):
        fd[i, 2].wait_recv()
        g = ys_g[i] + ry_g[i]
        gown[:, lanes(chunk_of(0, i))] = g[:, :128]
        gown[:, lanes(chunk_of(1, i))] = g[:, 128:]

    def reduce_y_f(i):
        fd[i, 3].wait_recv()
        f = ((pl_f[i, yl, c] + rc_f[i, yl]) + ry_f[i]).astype(BF16)
        fp[:, lanes(chunk_of(0, i))] = f[:, :128]
        fp[:, lanes(chunk_of(1, i))] = f[:, 128:]

    start_ph1(0, src=dt_hbm)
    yh_copy = send(dt_hbm, w.at[own_b], ga_send.at[0, 20], ga_recv.at[0, 20], yhp)
    start_ph2(0, 0, src=dt_hbm)

    scopy.wait()
    h1copy.wait()
    n_i = lax.broadcasted_iota(jnp.int32, (512, 512), 0)
    r_i = lax.broadcasted_iota(jnp.int32, (512, 512), 1)
    swapped = ((n_i // 32) % 4) * 128 + (n_i // 128) * 32 + n_i % 32
    perm[...] = (r_i == swapped).astype(F32).astype(BF16)
    eye[...] = (r_i == n_i).astype(F32).astype(BF16)
    yh_copy.wait_recv()
    start_ph1(1)
    start_ph2(1, 0)
    dcopy.wait()
    sp[0:512] = s[0:512]
    for a in range(4):
        for b in range(4):
            sp[512 + a * 128 + b * 32:512 + a * 128 + b * 32 + 32] = s[512 + b * 128 + a * 32:512 + b * 128 + a * 32 + 32]
    hh, hl = split(h1[...])
    h1h[:, :512] = hh[:, :512]
    h1l[:, :512] = hl[:, :512]
    h1h[:, 512:] = dot(hh[:, 512:], perm[...]).astype(BF16)
    h1l[:, 512:] = dot(hl[:, 512:], perm[...]).astype(BF16)

    fwd_ph1(0)
    fwd_ph2(0, 0)
    fwd_ph1(1)
    fwd_ph2(1, 0)
    for i in (1, 2):
        start_ph2(0, i)
        start_ph2(1, i)
    end_ph1(0)
    end_ph1(1)
    end_ph2(0, 0)
    end_ph2(1, 0)
    acopy.wait()
    group(0)
    start_ph2(0, 3)
    start_ph2(1, 3)
    fwd_ph2(0, 1)
    fwd_ph2(1, 1)
    reduce_core_g(0)
    reduce_core_f(0)
    st[...] = s[...].astype(F32).T.astype(BF16)
    end_ph2(0, 1)
    end_ph2(1, 1)
    group(1)
    fwd_ph2(0, 2)
    fwd_ph2(1, 2)
    reduce_y_g(0)
    reduce_y_f(0)
    reduce_core_g(1)
    reduce_core_f(1)
    end_ph2(0, 2)
    end_ph2(1, 2)
    group(2)
    fwd_ph2(0, 3)
    fwd_ph2(1, 3)
    reduce_y_g(1)
    reduce_y_f(1)
    reduce_core_g(2)
    reduce_core_f(2)
    end_ph2(0, 3)
    end_ph2(1, 3)
    group(3)
    reduce_core_g(3)
    reduce_y_g(2)
    reduce_y_g(3)

    def dot2(a, b):
        ah, al = split(a)
        return dot(ah, b) + dot(al, b)

    gsb[c, x, z] = dot2(gown[...], sp[...])
    gb[c, x, z] = gown[...]

    def gather_ph1(buf, half, ss, rs):
        cps = []
        for d in (1, 3, 2):
            a = buf.at[c, x, z, :, pl.ds(0, half)]
            b = buf.at[c, x, z, :, pl.ds(half, half)]
            cps.append(send(a, a, ss.at[d - 1], rs.at[d - 1], xdev(d)))
            cps.append(send(b, b, ss.at[3 + d - 1], rs.at[3 + d - 1], zdev(d)))
        return cps

    def gather_ph2(buf, half, ss, rs):
        cps = []
        for d in (1, 3, 2):
            a = buf.at[c, :, z, :, pl.ds(0, half)]
            b = buf.at[c, x, :, :, pl.ds(half, half)]
            cps.append(send(a, a, ss.at[6 + d - 1], rs.at[6 + d - 1], zdev(d)))
            cps.append(send(b, b, ss.at[9 + d - 1], rs.at[9 + d - 1], xdev(d)))
        return cps

    def gather_core(buf, ss, rs):
        return send(buf.at[c], buf.at[c], ss.at[12], rs.at[12], core)

    def wait_all(cps):
        for cp in cps:
            cp.wait_recv()

    g1 = gather_ph1(gsb, 128, gs_send, gs_recv)
    reduce_core_f(3)
    h2copy.wait()
    reduce_y_f(2)
    wait_all(g1)
    g2 = gather_ph2(gsb, 128, gs_send, gs_recv)
    gg1 = gather_ph1(gb, 512, gg_send, gg_recv)
    reduce_y_f(3)
    fn[:, :512] = fp[:, :512]
    fn[:, 512:] = dot(fp[:, 512:], perm[...]).astype(BF16)
    ft[:512] = dot(eye[...], fp[:, :512], NT).astype(BF16)
    ft[512:] = dot(perm[...], fp[:, 512:], NT).astype(BF16)
    proj = dot(fp[...], sp[...])
    wait_all(g2)
    g3 = gather_core(gsb, gs_send, gs_recv)
    wait_all(gg1)
    gg2 = gather_ph2(gb, 512, gg_send, gg_recv)
    g3.wait_recv()

    width = h2.shape[1]
    gs = gsb[...].reshape(1024, width)
    gsh, gsl = split(gs)
    inner = dot(st[...], gsh) + dot(st[...], gsl)
    ip, im = pos_neg(inner)
    h2v = h2[...]
    h2s = split(h2v)
    num = jnp.maximum(proj, 0.0) + dot3(h2s, im)
    den = jnp.maximum(-proj, 0.0) + dot3(h2s, ip)
    second_v[...] = h2v * jnp.sqrt(num / den)
    second_copy = pltpu.make_async_copy(second_v, second_hbm, local_sem.at[5])
    second_copy.start()

    def grad_body(j, carry):
        sn = split(second_v[...])
        rows = gsb[j // 2, pl.ds((j % 2) * 2, 2)].reshape(256, width)
        res = dot3(split(rows), sn, NT) - ft[pl.ds(pl.multiple_of(j * 256, 256), 256), :].astype(F32)
        g = dot3(split(res), sn)
        gp[0, j // 2, pl.ds((j % 2) * 2, 2)] = g[:, :128].reshape(2, 4, 32, 128)
        gp[1, j // 2, pl.ds((j % 2) * 2, 2)] = g[:, 128:].reshape(2, 4, 32, 128)
        return carry

    lax.fori_loop(0, 4, grad_body, 0)
    k1 = send(gp.at[1 - c], rcgp, rs_send.at[0], rs_recv.at[0], core)
    wait_all(gg2)
    gg3 = gather_core(gb, gg_send, gg_recv)
    k1.wait_recv()
    gs1[...] = gp[c] + rcgp[...]
    k2 = []
    for d in (1, 3, 2):
        k2.append(send(gs1.at[0, (x + d) % 4], r1a.at[d - 1], rs_send.at[d], rs_recv.at[d], xdev(d)))
        k2.append(send(gs1.at[1, :, (z + d) % 4], r1b.at[d - 1], rs_send.at[3 + d], rs_recv.at[3 + d], zdev(d)))
    gg3.wait_recv()

    def first_chunk(j):
        rows = gb[j // 2, pl.ds((j % 2) * 2, 2)].reshape(256, 1024)
        gpos, gneg = pos_neg(rows)
        hs = (h1h[...], h1l[...])
        cols = pl.ds(pl.multiple_of(j * 256, 256), 256)
        f = fn[:, cols].astype(F32)
        num_ = jnp.maximum(f, 0.0) + dot3(hs, gneg, NT)
        den_ = jnp.maximum(-f, 0.0) + dot3(hs, gpos, NT)
        first_v[:, cols] = h1[:, cols] * jnp.sqrt(num_ / den_)

    wait_all(k2)
    ab2[0] = (gs1[0, x] + r1a[0]) + (r1a[1] + r1a[2])
    ab2[1] = (gs1[1, :, z] + r1b[0]) + (r1b[1] + r1b[2])
    k3 = []
    for d in (1, 3, 2):
        k3.append(send(ab2.at[0, (z + d) % 4], r2a.at[d - 1], rs_send.at[6 + d], rs_recv.at[6 + d], zdev(d)))
        k3.append(send(ab2.at[1, (x + d) % 4], r2b.at[d - 1], rs_send.at[9 + d], rs_recv.at[9 + d], xdev(d)))
    wait_all(k3)
    ab3[0] = (ab2[0, z] + r2a[0]) + (r2a[1] + r2a[2])
    ab3[1] = (ab2[1, x] + r2b[0]) + (r2b[1] + r2b[2])
    k4 = []
    for d in (1, 3, 2):
        k4.append(send(ab3.at[((y + d) % 4) // 2], r3.at[d - 1], rs_send.at[12 + d], rs_recv.at[12 + d], ydev(d)))
    wait_all(k4)
    own = (ab3[yh] + r3[0]) + (r3[1] + r3[2])
    dirh[c] = own
    k5 = send(dirh.at[c], dirh.at[c], rs_send.at[16], rs_recv.at[16], core)

    sq = own * own
    nrm[0] = (sq[0:8] + sq[8:16]) + (sq[16:24] + sq[24:32])
    n1 = [send(nrm.at[0], nrx.at[d - 1], no_send.at[d - 1], no_recv.at[d - 1], xdev(d)) for d in (1, 3, 2)]
    wait_all(n1)
    nrm[1] = (nrm[0] + nrx[0]) + (nrx[1] + nrx[2])
    n2 = [send(nrm.at[1], nrz.at[d - 1], no_send.at[2 + d], no_recv.at[2 + d], zdev(d)) for d in (1, 3, 2)]
    wait_all(n2)
    nrm[2] = (nrm[1] + nrz[0]) + (nrz[1] + nrz[2])
    n3 = send(nrm.at[2], nry, no_send.at[6], no_recv.at[6], yhp)
    n3.wait_recv()
    nrm[3] = nrm[2] + nry[...]
    n4 = send(nrm.at[3], nrc, no_send.at[7], no_recv.at[7], core)
    n4.wait_recv()
    total = jnp.sum(nrm[3] + nrc[...])
    scale = jnp.sqrt(total / (1024 * width) + 1e-06)
    k5.wait_recv()
    dirf[:, :128] = dirh[0] / scale
    dirf[:, 128:] = dirh[1] / scale
    dir_copy = pltpu.make_async_copy(dirf, dir_hbm, local_sem.at[6])
    dir_copy.start()

    def first_body(j, carry):
        first_chunk(j)
        return carry

    lax.fori_loop(0, 4, first_body, 0)
    first_copy = pltpu.make_async_copy(first_v, first_hbm, local_sem.at[7])
    first_copy.start()
    for cp in pending:
        cp.wait_send()
    second_copy.wait()
    dir_copy.wait()
    first_copy.wait()


def shards(activations, dictionary, second_factor, first_codes, second_codes):
    tokens, rows = activations.shape
    sub, k1 = first_codes.shape[2:]
    k2 = second_codes.shape[3]
    v, dma = pltpu.VMEM, pltpu.SemaphoreType.DMA
    scratch = [
        v((tokens, rows), BF16), v((32, 32, rows), BF16), v((k1, k2), BF16), v((sub, k1), F32), v((sub, k2), F32),
        v((4, 2, 2, sub, 256), F32), v((4, 2, 32, 256), F32),
        v((4, 2, sub, 256), F32), v((4, 32, 256), F32),
        v((4, sub, 256), F32), v((4, 32, 256), F32),
        v((4, sub, 256), F32), v((4, 32, 256), F32),
        v((sub, k1), BF16), v((32, k1), F32), v((k1, k2), BF16), v((k2, k1), BF16),
        v((512, 512), BF16), v((512, 512), BF16), v((sub, k1), BF16), v((sub, k1), BF16),
        v((sub, k1), BF16), v((k1, sub), BF16),
        v((2, 4, 4, 32, k2), F32), v((2, 4, 4, 32, k1), F32), v((sub, k1), F32), v((sub, k2), F32),
        v((2, 2, 4, 4, 32, 128), F32), v((2, 4, 4, 32, 128), F32), v((2, 4, 4, 32, 128), F32),
        v((3, 4, 32, 128), F32), v((3, 4, 32, 128), F32), v((2, 4, 32, 128), F32),
        v((3, 32, 128), F32), v((3, 32, 128), F32), v((2, 32, 128), F32), v((3, 32, 128), F32),
        v((2, 32, 128), F32), v((32, 256), F32),
        v((4, 8, 128), F32), v((3, 8, 128), F32), v((3, 8, 128), F32), v((8, 128), F32), v((8, 128), F32),
        dma((8,)), dma((2, 21)), dma((2, 21)), dma((4, 4)), dma((4, 4)), dma((13,)), dma((13,)), dma((13,)), dma((13,)),
        dma((17,)), dma((17,)), dma((8,)), dma((8,)),
    ]
    hbm = pl.BlockSpec(memory_space=pl.ANY)
    first, second, direction = pl.pallas_call(
        kernel,
        out_shape=(
            jax.ShapeDtypeStruct((sub, k1), F32),
            jax.ShapeDtypeStruct((sub, k2), F32),
            jax.ShapeDtypeStruct((32, k2), F32),
        ),
        in_specs=[hbm] * 5,
        out_specs=(hbm,) * 3,
        scratch_shapes=scratch,
        compiler_params=pltpu.CompilerParams(
            collective_id=0, has_side_effects=True, vmem_limit_bytes=60 * 1024 * 1024
        ),
        name="sweep",
    )(activations, dictionary.T, second_factor, first_codes.reshape(sub, k1), second_codes.reshape(sub, k2))
    return first.reshape(first_codes.shape), second.reshape(second_codes.shape), direction


def solution(mesh):
    in_specs = (
        P("tok", "hid"),
        P("hid", "tok"),
        P(),
        P("tok", "hid", None, None),
        P("tok", "hid", None, None),
    )
    out_specs = (P("tok", "hid", None, None), P("tok", "hid", None, None), P("tok", None))
    return jax.shard_map(shards, mesh=mesh, in_specs=in_specs, out_specs=out_specs, check_vma=False)
```

time: 600 us -> 126 us (0.21); the launches traced: 588 us -> 125 us
  waiting for transfers between devices: 446 us -> 0 us
  Pallas kernels: 0 us -> 119 us
  blocking collectives: 81.1 us -> 0 us
  matrix products: 44.3 us -> 0 us
  between operations: 14.6 us -> 0.64 us
    psum x2 -> x0, waiting for transfers between devices: 230 us -> none  [the longest x1 137 us: shards(): cross_all, codegram = lax.psum((cross_part, codegram_part), ('hid', 'tok'))]
    all_gather x2 -> x0, waiting for transfers between devices: 168 us -> none  [the longest x1 104 us: shards(): whole_rows = lax.all_gather(dictionary, 'tok', axis=1, tiled=True)]
    pallas_call x0 -> x1, Pallas kernels: none -> 119 us  [shards(): pl.pallas_call(kernel, out_shape=(jax.ShapeDtypeStruct((sub, k1), F32), j...]
    psum x1 -> x0, blocking collectives: 81.1 us -> none  [shards(): squares = lax.psum(jnp.sum(grad * grad), 'tok')]
    reduce_scatter x1 -> x0, waiting for transfers between devices: 46.1 us -> none  [shards(): lax.psum_scatter(feat_part, 'hid', scatter_dimension=0, tiled=True)]
    dot_general x13 -> x0, matrix products: 44.3 us -> none  [the longest x1 13.5 us: shards(): jnp.dot(activations, whole_rows, preferred_element_type=jnp.float32)]
  transfers between devices with their start and end apart: 5 -> 0, of which waited for: 5 -> 0; matrix products, arithmetic and copies ran while one was open for 5% -> 0% of each run, Pallas kernels for 0% -> 0%
where the time goes in v1:
time: 126 us; the launch traced here: 125 us
  Pallas kernels  119 us (94%)
  local copies, waits for them, and re-layouts  5.35 us (4%)
    pallas_call x1, Pallas kernels, shards(): pl.pallas_call(kernel, out_shape=(jax.ShapeDtypeStruct((sub, k1), F32), j...  119 us
    unnamed x3, local copies, waits for them, and re-layouts  5.35 us

profile of v1, /device:TPU:1, one launch (start us, length us, event | category | flops | bytes accessed | tf_op | source)
XLA Modules:
  0.0 125.4 jit_solution(16133329948456366779)
XLA Ops:
  0.6 119.4 %sweep.1 = (f32[256,1024]{1,0:T(8,128)}, f32[256,256]{1,0:T(8,128)}, f32[32,256]{1,0:T(8,128)}) custom-call(bf16[1024,3584]{1,0:T(8,128)(2,1)} %act_hbm.1, bf16[32,3584]{1,0:T(8,128)(2,1)} %bitcast.9, bf16[1024,256]{1,0:T(8,128)(2,1)} %s_hbm.1, f32[256,1024]{1,0:T(8,128)} %bitcast.5, f32[256,256]{1,0:T(8,128)} %bitcast.7), custom_call_target="tpu_custom_call" | custom-call | tf_op jit(solution)/shard_map/sweep/pallas_call | solution.py:457
  120.0 2.3 %copy.11 = f32[1,1,256,1024]{3,2,1,0:T(8,128)} copy(f32[1,1,256,1024]{3,2,1,0:T(8,128)} %bitcast.6) | data formatting | bytes 2097152
  122.3 1.7 %copy.12 = f32[1,1,256,256]{3,2,1,0:T(8,128)} copy(f32[1,1,256,256]{3,2,1,0:T(8,128)} %bitcast.8) | data formatting | bytes 524288
  124.0 1.4 %copy.13 = f32[32,256]{1,0:T(8,128)} copy(f32[32,256]{1,0:T(8,128)} %get-tuple-element.14) | data formatting | bytes 65536

commit v2 on v0

v2 whole, which is shorter than its diff:
```python
import functools

import jax
import jax.numpy as jnp
from jax import lax
from jax.experimental import pallas as pl
from jax.experimental.pallas import tpu as pltpu
from jax.sharding import PartitionSpec as P

F32 = jnp.float32
BF16 = jnp.bfloat16
MESH = pl.DeviceIdType.MESH
NN = (((1,), (0,)), ((), ()))
NT = (((1,), (1,)), ((), ()))


def dot(a, b, dims=NN):
    return lax.dot_general(a, b, dims, preferred_element_type=F32)


def split(a):
    hi = a.astype(BF16)
    return hi, (a - hi.astype(F32)).astype(BF16)


def dot3(a, b, dims=NN):
    ah, al = a
    bh, bl = b
    return dot(ah, bh, dims) + (dot(al, bh, dims) + dot(ah, bl, dims))


def pos_neg(g):
    p = split(jnp.maximum(g, 0.0))
    n = split(jnp.maximum(-g, 0.0))
    return p, n


ORDER = (
    (2, 1), (0, 2, 0, 1, 1), (0, 2, 0, 0, 1), (0, 1, 0, 1), (0, 1, 1, 1), (0, 2, 0, 1, 0), (0, 1, 0, 0),
    (0, 2, 0, 0, 0), (2, 0), (0, 1, 1, 0), (4, 0), (4, 1), (1, 1, 0, 1), (1, 1, 1, 1), (1, 2, 0, 0, 1), (0, 1, 2, 1),
    (1, 2, 0, 1, 1), (1, 1, 0, 0), (1, 1, 1, 0), (0, 2, 2, 1, 1), (1, 2, 0, 0, 0), (0, 1, 2, 0), (0, 2, 1, 0, 0),
    (0, 2, 1, 1, 1), (0, 2, 0, 2, 1), (0, 2, 0, 2, 0), (1, 2, 1, 1, 1), (1, 1, 2, 1), (1, 2, 0, 1, 0),
    (0, 2, 1, 0, 1), (1, 2, 1, 0, 0), (1, 2, 0, 2, 0), (1, 2, 0, 2, 1), (1, 2, 2, 0, 0), (1, 2, 1, 0, 1),
    (1, 2, 2, 1, 1), (0, 2, 2, 0, 0), (0, 2, 1, 1, 0), (4, 2), (1, 2, 1, 2, 1), (1, 2, 1, 2, 0), (0, 2, 1, 2, 0),
    (3, 0, 0), (1, 1, 2, 0), (1, 2, 1, 1, 0), (0, 2, 1, 2, 1), (0, 2, 2, 0, 1), (1, 2, 2, 0, 1), (3, 0, 1),
    (1, 2, 2, 2, 1), (0, 2, 2, 1, 0), (0, 2, 2, 2, 0), (1, 2, 2, 2, 0), (1, 2, 2, 1, 0), (0, 2, 2, 2, 1),
    (0, 2, 3, 1, 1), (3, 0, 2), (0, 2, 3, 0, 0), (3, 0, 3), (0, 2, 3, 0, 1), (3, 1, 0), (0, 2, 3, 1, 0),
    (1, 2, 3, 0, 0), (1, 2, 3, 1, 1), (1, 2, 3, 1, 0), (1, 2, 3, 0, 1), (3, 1, 1), (3, 1, 2), (3, 1, 3), (3, 2, 0),
    (0, 2, 3, 2, 1), (0, 2, 3, 2, 0), (1, 2, 3, 2, 0), (1, 2, 3, 2, 1), (3, 2, 1), (3, 2, 2), (3, 2, 3), (3, 3, 0),
    (3, 3, 1), (3, 3, 2), (3, 3, 3),
)


def kernel(
    act_hbm, dt_hbm, s_hbm, h1_hbm, h2_hbm,
    first_hbm, second_hbm, dir_hbm,
    act, w, s, h1, h2,
    pl_f, pl_g, rc_f, rc_g, ys_f, ry_f,
    fp, gown, sp, st, perm, eye, h1h, h1l, fn, ft,
    gsb, gb, dg, first_v, second_v,
    gp, rcgp, gs1, r1a, r1b, ab2, r2a, r2b, ab3, r3, fin, dirh, dirf,
    nrm, nrr, nrc,
    local_sem, ga_send, ga_recv, fe_send, fe_recv, gs_send, gs_recv, gg_send, gg_recv,
    dg_send, dg_recv, rs_send, rs_recv, no_send, no_recv,
):
    hid = lax.axis_index("hid")
    tok = lax.axis_index("tok")
    yl, c = hid // 2, hid % 2
    yh, x, z = tok // 16, (tok // 4) % 4, tok % 4
    y = yh * 2 + yl
    sub = h1.shape[0]
    width = h2.shape[1]

    def dev(yl_, c_, yh_, x_, z_):
        return (yl_ * 2 + c_, yh_ * 16 + x_ * 4 + z_)

    core = dev(yl, 1 - c, yh, x, z)
    ylp = dev(1 - yl, c, yh, x, z)
    ylc = dev(1 - yl, 1 - c, yh, x, z)
    yhp = dev(yl, c, 1 - yh, x, z)

    def plane(dx, dz):
        return dev(yl, c, yh, (x + dx) % 4, (z + dz) % 4)

    def xdev(d):
        return plane(d, 0)

    def zdev(d):
        return plane(0, d)

    def ydev(d):
        yy = (y + d) % 4
        return dev(yy % 2, c, yy // 2, x, z)

    own_b = yh * 16 + x * 4 + z
    dcopy = pltpu.make_async_copy(dt_hbm, w.at[own_b], local_sem.at[1])
    dcopy.start()
    scopy = pltpu.make_async_copy(s_hbm, s, local_sem.at[2])
    scopy.start()
    h1copy = pltpu.make_async_copy(h1_hbm, h1, local_sem.at[3])
    h1copy.start()
    h2copy = pltpu.make_async_copy(h2_hbm, h2, local_sem.at[4])
    h2copy.start()
    acopy = pltpu.make_async_copy(act_hbm, act, local_sem.at[0])
    acopy.start()

    barrier = pltpu.get_barrier_semaphore()
    peers = [plane(dx, dz) for dx in range(4) for dz in range(4) if dx + dz > 0]
    peers += [ydev(1), ydev(2), ydev(3), core, ylc]
    for who in peers:
        pl.semaphore_signal(barrier, inc=1, device_id=who, device_id_type=MESH)
    pl.semaphore_wait(barrier, len(peers))

    pending = []

    def send(src, dst, ss, rs, who):
        cp = pltpu.make_async_remote_copy(
            src_ref=src, dst_ref=dst, send_sem=ss, recv_sem=rs, device_id=who, device_id_type=MESH
        )
        cp.start()
        pending.append(cp)
        return cp

    def settle():
        for cp in pending:
            cp.wait_send()
        pending.clear()

    def wait_all(cps):
        for cp in cps:
            cp.wait_recv()

    def part(o):
        p = (yh + o) % 2
        u = x + p * (z - x)
        v = z + p * (x - z)
        return p, u, v

    def blk(p, u_, v_):
        return p * 16 + u_ * (4 - 3 * p) + v_ * (1 + 3 * p)

    DU = (0, 3, 1, 2)

    def gdev(o, du, dv):
        p, u, v = part(o)
        u_, v_ = (u + du) % 4, (v + dv) % 4
        return (hid, yh * 16 + u_ * (4 - 3 * p) + v_ * (1 + 3 * p))

    def gblk(o, du, dv):
        p, u, v = part(o)
        return blk(p, (u + du) % 4, (v + dv) % 4)

    gd = {}
    arrived = set()

    def need(*key):
        if key not in arrived:
            arrived.add(key)
            gd[key].wait_recv()

    def gsend(key, k, b, who, r, hbm=False):
        o = key[0]
        dst = w.at[b, pl.ds(16 * r, 16)]
        src = dt_hbm.at[pl.ds(16 * r, 16)] if hbm else dst
        gd[key] = send(src, dst, ga_send.at[o, k], ga_recv.at[o, k], who)

    def own_here(o, r):
        if o == 1:
            need(2, r)

    def step(key):
        o = key[0]
        if o == 2:
            gsend(key, key[1], own_b, yhp, key[1], True)
        elif key[1] == 1:
            _, _, sg, r = key
            if sg < 2:
                own_here(o, r)
                gsend(key, sg * 2 + r, gblk(o, 0, 0), gdev(o, 3 if sg else 1, 0), r, o == 0)
            else:
                need(o, 1, r, r)
                gsend(key, 4 + r, gblk(o, 1 if r else 3, 0), gdev(o, 3 if r else 1, 0), r)
        else:
            _, _, i, sg, r = key
            k = 6 + 6 * i
            if sg < 2:
                if i == 0:
                    own_here(o, r)
                elif i < 3:
                    need(o, 1, i - 1, r)
                else:
                    need(o, 1, 2, r)
                gsend(key, k + sg * 2 + r, gblk(o, DU[i], 0), gdev(o, 0, 3 if sg else 1), r, o == 0 and i == 0)
            else:
                need(o, 2, i, r, r)
                gsend(key, k + 4 + r, gblk(o, DU[i], 1 if r else 3), gdev(o, 0, 3 if r else 1), r)

    def need_group(i):
        for o in (0, 1):
            for r in (0, 1):
                own_here(o, r)
                if i in (1, 2):
                    need(o, 1, i - 1, r)
                if i == 3:
                    need(o, 1, 2, r)
                for sg in (0, 1, 2):
                    need(o, 2, i, sg, r)

    fd = {}

    def chunk_of(o, i):
        p, u, v = part(o)
        return p * 4 + (u + DU[i]) % 4

    def weights(i):
        rows = []
        for o in (0, 1):
            p, u, v = part(o)
            rows += [w[blk(p, (u + DU[i]) % 4, j)] for j in range(4)]
        return jnp.concatenate(rows, axis=0)

    def group_g(i):
        need_group(i)
        lrows = jnp.concatenate([w[x * 4 + z], w[16 + x * 4 + z]], axis=0)
        g = dot(lrows, weights(i), NT)
        pl_g[i] = g.reshape(2, 32, g.shape[1])
        fd[i, 0] = send(pl_g.at[i, 1 - c], rc_g.at[i, 0], fe_send.at[i, 0], fe_recv.at[i, 0], core)
        fd[i, 1] = send(pl_g.at[i, c], rc_g.at[i, 1], fe_send.at[i, 1], fe_recv.at[i, 1], ylp)
        fd[i, 2] = send(pl_g.at[i, 1 - c], rc_g.at[i, 2], fe_send.at[i, 2], fe_recv.at[i, 2], ylc)

    def group_f(i, other):
        cc = 1 - c if other else c
        a = act[:, cc].reshape(2 * sub, act.shape[3])
        pl_f[i, cc] = dot(a, weights(i), NT).reshape(2, sub, 256)
        if other:
            fd[i, 3] = send(pl_f.at[i, cc], rc_f.at[i], fe_send.at[i, 3], fe_recv.at[i, 3], core)

    def reduce_core(i):
        fd[i, 3].wait_recv()
        ys_f[i] = pl_f[i, c, 1 - yl] + rc_f[i, 1 - yl]
        fd[i, 4] = send(ys_f.at[i], ry_f.at[i], fe_send.at[i, 4], fe_recv.at[i, 4], ylp)

    def lanes(q):
        return pl.ds(pl.multiple_of(q * 128, 128), 128)

    def reduce_g(i):
        for k in range(3):
            fd[i, k].wait_recv()
        g = (pl_g[i, c] + rc_g[i, 0]) + (rc_g[i, 1] + rc_g[i, 2])
        gown[:, lanes(chunk_of(0, i))] = g[:, :128]
        gown[:, lanes(chunk_of(1, i))] = g[:, 128:]

    def reduce_f(i):
        fd[i, 4].wait_recv()
        f = ((pl_f[i, c, yl] + rc_f[i, yl]) + ry_f[i]).astype(BF16)
        fp[:, lanes(chunk_of(0, i))] = f[:, :128]
        fp[:, lanes(chunk_of(1, i))] = f[:, 128:]

    def prepare_a():
        n_i = lax.broadcasted_iota(jnp.int32, (512, 512), 0)
        r_i = lax.broadcasted_iota(jnp.int32, (512, 512), 1)
        swapped = ((n_i // 32) % 4) * 128 + (n_i // 128) * 32 + n_i % 32
        perm[...] = (r_i == swapped).astype(F32).astype(BF16)
        eye[...] = (r_i == n_i).astype(F32).astype(BF16)

    def prepare_b():
        scopy.wait()
        sp[0:512] = s[0:512]
        for a in range(4):
            for b in range(4):
                to, at = 512 + a * 128 + b * 32, 512 + b * 128 + a * 32
                sp[to:to + 32] = s[at:at + 32]
        st[...] = s[...].astype(F32).T.astype(BF16)

    def prepare_c():
        h1copy.wait()
        hh, hl = split(h1[...])
        h1h[:, :512] = hh[:, :512]
        h1l[:, :512] = hl[:, :512]
        h1h[:, 512:] = dot(hh[:, 512:], perm[...]).astype(BF16)
        h1l[:, 512:] = dot(hl[:, 512:], perm[...]).astype(BF16)

    for op in ORDER:
        if op[0] < 3:
            step(op)
        elif op[0] == 3:
            _, i, k = op
            if k == 0:
                if i == 0:
                    dcopy.wait()
                    acopy.wait()
                group_g(i)
            elif k < 3:
                group_f(i, k == 1)
            else:
                if i < 3:
                    reduce_core(i)
                if i > 0:
                    reduce_g(i - 1)
                if i in (1, 2):
                    reduce_f(i - 1)
        else:
            (prepare_a, prepare_b, prepare_c)[op[1]]()
    reduce_g(3)

    g = gown[...]
    gh, gl = split(g)
    gsb[c, x, z] = dot(gh, sp[...]) + dot(gl, sp[...])

    half = width // 2

    def gs_core(ref, k):
        return send(ref, ref, gs_send.at[k], gs_recv.at[k], core)

    g1 = []
    for d in (1, 3, 2):
        a = gsb.at[c, x, z, :, pl.ds(0, half)]
        b = gsb.at[c, x, z, :, pl.ds(half, half)]
        g1.append(send(a, a, gs_send.at[d - 1], gs_recv.at[d - 1], xdev(d)))
        g1.append(send(b, b, gs_send.at[3 + d - 1], gs_recv.at[3 + d - 1], zdev(d)))

    reduce_core(3)

    at_diag = c * 512 + (x + c * (z - x)) * 128 + (z + c * (x - z)) * 32
    lane = lax.broadcasted_iota(jnp.int32, g.shape, 1)
    row = lax.broadcasted_iota(jnp.int32, g.shape, 0)
    on = lane == at_diag + row
    gb[c, x, z] = jnp.where(on, 0.0, g).astype(BF16)
    dg[c, x, z] = jnp.broadcast_to(jnp.sum(jnp.where(on, g, 0.0), axis=1, keepdims=True), (32, 128))

    wait_all(g1)
    g2 = []
    for d in (1, 3, 2):
        a = gsb.at[c, :, z, :, pl.ds(0, half)]
        b = gsb.at[c, x, :, :, pl.ds(half, half)]
        g2.append((d, 0, send(a, a, gs_send.at[6 + d - 1], gs_recv.at[6 + d - 1], zdev(d))))
        g2.append((d, 1, send(b, b, gs_send.at[9 + d - 1], gs_recv.at[9 + d - 1], xdev(d))))
    g3 = [
        gs_core(gsb.at[c, :, z, :, pl.ds(0, half)], 12),
        gs_core(gsb.at[c, x, :, :, pl.ds(half, half)], 13),
    ]
    gg1 = []
    for d in (1, 3, 2):
        a = gb.at[c, x, z, :, pl.ds(0, 512)]
        b = gb.at[c, x, z, :, pl.ds(512, 512)]
        e = dg.at[c, x, z]
        gg1.append(send(a, a, gg_send.at[d - 1], gg_recv.at[d - 1], xdev(d)))
        gg1.append(send(b, b, gg_send.at[3 + d - 1], gg_recv.at[3 + d - 1], zdev(d)))
        gg1.append(send(e, e, dg_send.at[d - 1], dg_recv.at[d - 1], xdev(d)))
    reduce_f(2)
    for d, o, cp in g2:
        cp.wait_recv()
        if o == 0:
            g3.append(gs_core(gsb.at[c, :, (z + 4 - d) % 4, :, pl.ds(0, half)], 14 + d))
        else:
            g3.append(gs_core(gsb.at[c, (x + 4 - d) % 4, :, :, pl.ds(half, half)], 17 + d))
    reduce_f(3)
    fn[:, :512] = fp[:, :512]
    fn[:, 512:] = dot(fp[:, 512:], perm[...]).astype(BF16)
    ft[:512] = dot(eye[...], fp[:, :512], NT).astype(BF16)
    ft[512:] = dot(perm[...], fp[:, 512:], NT).astype(BF16)
    proj = dot(fp[...], sp[...])
    wait_all(gg1)
    gg2 = []
    for d in (1, 3, 2):
        a = gb.at[c, :, z, :, pl.ds(0, 512)]
        b = gb.at[c, x, :, :, pl.ds(512, 512)]
        e = dg.at[c, :, z]
        gg2.append(send(a, a, gg_send.at[6 + d - 1], gg_recv.at[6 + d - 1], zdev(d)))
        gg2.append(send(b, b, gg_send.at[9 + d - 1], gg_recv.at[9 + d - 1], xdev(d)))
        gg2.append(send(e, e, dg_send.at[3 + d - 1], dg_recv.at[3 + d - 1], zdev(d)))
    h2copy.wait()
    wait_all(g3)

    gs = gsb[...].reshape(1024, width)
    gsh, gsl = split(gs)
    inner = dot(st[...], gsh) + dot(st[...], gsl)
    ip, im = pos_neg(inner)
    h2v = h2[...]
    h2s = split(h2v)
    num = jnp.maximum(proj, 0.0) + dot3(h2s, im)
    den = jnp.maximum(-proj, 0.0) + dot3(h2s, ip)
    second_v[...] = h2v * jnp.sqrt(num / den)
    second_copy = pltpu.make_async_copy(second_v, second_hbm, local_sem.at[5])
    second_copy.start()

    def grad_body(j, carry):
        sn = split(second_v[...])
        rows = gsb[j // 2, pl.ds((j % 2) * 2, 2)].reshape(256, width)
        res = dot3(split(rows), sn, NT) - ft[pl.ds(pl.multiple_of(j * 256, 256), 256), :].astype(F32)
        gr = dot3(split(res), sn)
        gp[0, j // 2, pl.ds((j % 2) * 2, 2)] = gr[:, :128].reshape(2, 4, 32, 128)
        gp[1, j // 2, pl.ds((j % 2) * 2, 2)] = gr[:, 128:].reshape(2, 4, 32, 128)
        return carry

    lax.fori_loop(0, 4, grad_body, 0)
    k1 = send(gp.at[1 - c], rcgp, rs_send.at[0], rs_recv.at[0], core)

    def first_body(j, carry):
        gt = gb[j // 2, pl.ds((j % 2) * 2, 2)].reshape(256, 1024)
        diag = dg[j // 2, pl.ds((j % 2) * 2, 2)].reshape(256, 128).T[0:1]
        gpos, gneg = jnp.maximum(gt, 0), jnp.maximum(-gt, 0)
        cols = pl.ds(pl.multiple_of(j * 256, 256), 256)
        f = fn[:, cols].astype(F32)
        h = h1[:, cols]
        num_ = jnp.maximum(f, 0.0) + (dot(h1h[...], gneg, NT) + dot(h1l[...], gneg, NT))
        den_ = jnp.maximum(-f, 0.0) + (dot(h1h[...], gpos, NT) + dot(h1l[...], gpos, NT)) + h * diag
        first_v[:, cols] = h * jnp.sqrt(num_ / den_)
        return carry

    k1.wait_recv()
    gs1[...] = gp[c] + rcgp[...]
    k2 = []
    for d in (1, 3, 2):
        k2.append(send(gs1.at[0, (x + d) % 4], r1a.at[d - 1], rs_send.at[d], rs_recv.at[d], xdev(d)))
        k2.append(send(gs1.at[1, :, (z + d) % 4], r1b.at[d - 1], rs_send.at[3 + d], rs_recv.at[3 + d], zdev(d)))
    wait_all(gg2)
    gg3 = [
        send(gb.at[c], gb.at[c], gg_send.at[12], gg_recv.at[12], core),
        send(dg.at[c], dg.at[c], dg_send.at[6], dg_recv.at[6], core),
    ]
    late = pending[-8:]
    del pending[-8:]
    settle()
    pending.extend(late)
    wait_all(k2)
    ab2[0] = (gs1[0, x] + r1a[0]) + (r1a[1] + r1a[2])
    ab2[1] = (gs1[1, :, z] + r1b[0]) + (r1b[1] + r1b[2])
    k3 = []
    for d in (1, 3, 2):
        k3.append(send(ab2.at[0, (z + d) % 4], r2a.at[d - 1], rs_send.at[6 + d], rs_recv.at[6 + d], zdev(d)))
        k3.append(send(ab2.at[1, (x + d) % 4], r2b.at[d - 1], rs_send.at[9 + d], rs_recv.at[9 + d], xdev(d)))
    wait_all(gg3)
    lax.fori_loop(0, 2, first_body, 0)
    wait_all(k3)
    ab3[0] = (ab2[0, z] + r2a[0]) + (r2a[1] + r2a[2])
    ab3[1] = (ab2[1, x] + r2b[0]) + (r2b[1] + r2b[2])
    k4 = []
    for d in (1, 3, 2):
        k4.append(send(ab3, r3.at[d - 1], rs_send.at[12 + d], rs_recv.at[12 + d], ydev(d)))
    lax.fori_loop(2, 4, first_body, 0)
    first_copy = pltpu.make_async_copy(first_v, first_hbm, local_sem.at[7])
    first_copy.start()
    wait_all(k4)
    fin[...] = (ab3[...] + r3[0]) + (r3[1] + r3[2])

    sq = fin[0] * fin[0] + fin[1] * fin[1]
    nrm[0] = (sq[0:8] + sq[8:16]) + (sq[16:24] + sq[24:32])
    n1 = []
    for dx in range(4):
        for dz in range(4):
            k = dx * 4 + dz - 1
            if k >= 0:
                n1.append(send(nrm.at[0], nrr.at[k], no_send.at[k], no_recv.at[k], plane(dx, dz)))
    dirh[c] = fin[yh]
    k5 = send(dirh.at[c], dirh.at[c], rs_send.at[16], rs_recv.at[16], core)
    wait_all(n1)
    nrm[1] = nrm[0] + jnp.sum(nrr[...], axis=0)
    n4 = send(nrm.at[1], nrc, no_send.at[15], no_recv.at[15], core)
    settle()
    k5.wait_recv()
    n4.wait_recv()
    total = jnp.sum(nrm[1] + nrc[...])
    scale = jnp.sqrt(total / (1024 * width) + 1e-06)
    dirf[:, :128] = dirh[0] / scale
    dirf[:, 128:] = dirh[1] / scale
    dir_copy = pltpu.make_async_copy(dirf, dir_hbm, local_sem.at[6])
    dir_copy.start()
    second_copy.wait()
    first_copy.wait()
    dir_copy.wait()


def shards(activations, dictionary, second_factor, first_codes, second_codes):
    tokens, rows = activations.shape
    sub, k1 = first_codes.shape[2:]
    k2 = second_codes.shape[3]
    v, dma = pltpu.VMEM, pltpu.SemaphoreType.DMA
    scratch = [
        v((2, 2, sub, rows), BF16), v((32, 32, rows), BF16), v((k1, k2), BF16), v((sub, k1), F32), v((sub, k2), F32),
        v((4, 2, 2, sub, 256), F32), v((4, 2, 32, 256), F32),
        v((4, 2, sub, 256), F32), v((4, 3, 32, 256), F32),
        v((4, sub, 256), F32), v((4, sub, 256), F32),
        v((sub, k1), BF16), v((32, k1), F32), v((k1, k2), BF16), v((k2, k1), BF16),
        v((512, 512), BF16), v((512, 512), BF16), v((sub, k1), BF16), v((sub, k1), BF16),
        v((sub, k1), BF16), v((k1, sub), BF16),
        v((2, 4, 4, 32, k2), F32), v((2, 4, 4, 32, k1), BF16), v((2, 4, 4, 32, 128), F32),
        v((sub, k1), F32), v((sub, k2), F32),
        v((2, 2, 4, 4, 32, 128), F32), v((2, 4, 4, 32, 128), F32), v((2, 4, 4, 32, 128), F32),
        v((3, 4, 32, 128), F32), v((3, 4, 32, 128), F32), v((2, 4, 32, 128), F32),
        v((3, 32, 128), F32), v((3, 32, 128), F32), v((2, 32, 128), F32), v((3, 2, 32, 128), F32),
        v((2, 32, 128), F32), v((2, 32, 128), F32), v((32, 256), F32),
        v((2, 8, 128), F32), v((15, 8, 128), F32), v((8, 128), F32),
        dma((8,)), dma((3, 30)), dma((3, 30)), dma((4, 5)), dma((4, 5)), dma((21,)), dma((21,)), dma((13,)), dma((13,)),
        dma((7,)), dma((7,)), dma((17,)), dma((17,)), dma((16,)), dma((16,)),
    ]
    hbm = pl.BlockSpec(memory_space=pl.ANY)
    first, second, direction = pl.pallas_call(
        kernel,
        out_shape=(
            jax.ShapeDtypeStruct((sub, k1), F32),
            jax.ShapeDtypeStruct((sub, k2), F32),
            jax.ShapeDtypeStruct((32, k2), F32),
        ),
        in_specs=[hbm] * 5,
        out_specs=(hbm,) * 3,
        scratch_shapes=scratch,
        compiler_params=pltpu.CompilerParams(
            collective_id=0, has_side_effects=True, vmem_limit_bytes=60 * 1024 * 1024
        ),
        name="sweep",
    )(activations.reshape(2, 2, sub, rows), dictionary.T, second_factor, first_codes.reshape(sub, k1), second_codes.reshape(sub, k2))
    return first.reshape(first_codes.shape), second.reshape(second_codes.shape), direction


def solution(mesh):
    in_specs = (
        P("tok", "hid"),
        P("hid", "tok"),
        P(),
        P("tok", "hid", None, None),
        P("tok", "hid", None, None),
    )
    out_specs = (P("tok", "hid", None, None), P("tok", "hid", None, None), P("tok", None))
    return jax.shard_map(shards, mesh=mesh, in_specs=in_specs, out_specs=out_specs, check_vma=False)
```

time: 600 us -> 107 us (0.18); the launches traced: 588 us -> 106 us
  waiting for transfers between devices: 446 us -> 0 us
  Pallas kernels: 0 us -> 100 us
  blocking collectives: 81.1 us -> 0 us
  matrix products: 44.3 us -> 0 us
  between operations: 14.6 us -> 0.64 us
    psum x2 -> x0, waiting for transfers between devices: 230 us -> none  [the longest x1 137 us: shards(): cross_all, codegram = lax.psum((cross_part, codegram_part), ('hid', 'tok'))]
    all_gather x2 -> x0, waiting for transfers between devices: 168 us -> none  [the longest x1 104 us: shards(): whole_rows = lax.all_gather(dictionary, 'tok', axis=1, tiled=True)]
    pallas_call x0 -> x1, Pallas kernels: none -> 100 us  [shards(): pl.pallas_call(kernel, out_shape=(jax.ShapeDtypeStruct((sub, k1), F32), j...]
    psum x1 -> x0, blocking collectives: 81.1 us -> none  [shards(): squares = lax.psum(jnp.sum(grad * grad), 'tok')]
    reduce_scatter x1 -> x0, waiting for transfers between devices: 46.1 us -> none  [shards(): lax.psum_scatter(feat_part, 'hid', scatter_dimension=0, tiled=True)]
    dot_general x13 -> x0, matrix products: 44.3 us -> none  [the longest x1 13.5 us: shards(): jnp.dot(activations, whole_rows, preferred_element_type=jnp.float32)]
  transfers between devices with their start and end apart: 5 -> 0, of which waited for: 5 -> 0; matrix products, arithmetic and copies ran while one was open for 5% -> 0% of each run, Pallas kernels for 0% -> 0%
where the time goes in v2:
time: 107 us; the launch traced here: 106 us
  Pallas kernels  100 us (93%)
  local copies, waits for them, and re-layouts  5.35 us (5%)
    pallas_call x1, Pallas kernels, shards(): pl.pallas_call(kernel, out_shape=(jax.ShapeDtypeStruct((sub, k1), F32), j...  100 us
    unnamed x3, local copies, waits for them, and re-layouts  5.35 us

profile of v2, /device:TPU:1, one launch (start us, length us, event | category | flops | bytes accessed | tf_op | source)
XLA Modules:
  0.0 106.3 jit_solution(6387088623987088335)
XLA Ops:
  0.6 100.3 %sweep.1 = (f32[256,1024]{1,0:T(8,128)}, f32[256,256]{1,0:T(8,128)}, f32[32,256]{1,0:T(8,128)}) custom-call(bf16[2,2,256,3584]{3,2,1,0:T(8,128)(2,1)} %bitcast.6, bf16[32,3584]{1,0:T(8,128)(2,1)} %bitcast.11, bf16[1024,256]{1,0:T(8,128)(2,1)} %s_hbm.1, f32[256,1024]{1,0:T(8,128)} %bitcast.7, f32[256,256]{1,0:T(8,128)} %bitcast.9), custom_call_target="tpu_custom_call" | custom-call | tf_op jit(solution)/shard_map/sweep/pallas_call | solution.py:498
  101.0 2.3 %copy.11 = f32[1,1,256,1024]{3,2,1,0:T(8,128)} copy(f32[1,1,256,1024]{3,2,1,0:T(8,128)} %bitcast.8) | data formatting | bytes 2097152
  103.3 1.7 %copy.12 = f32[1,1,256,256]{3,2,1,0:T(8,128)} copy(f32[1,1,256,256]{3,2,1,0:T(8,128)} %bitcast.10) | data formatting | bytes 524288
  104.9 1.4 %copy.13 = f32[32,256]{1,0:T(8,128)} copy(f32[32,256]{1,0:T(8,128)} %get-tuple-element.14) | data formatting | bytes 65536

commit v3 on v2

--- a/solution.py
+++ b/solution.py
@@ -36,18 +36,17 @@
 
 
 ORDER = (
-    (2, 1), (0, 2, 0, 1, 1), (0, 2, 0, 0, 1), (0, 1, 0, 1), (0, 1, 1, 1), (0, 2, 0, 1, 0), (0, 1, 0, 0),
-    (0, 2, 0, 0, 0), (2, 0), (0, 1, 1, 0), (4, 0), (4, 1), (1, 1, 0, 1), (1, 1, 1, 1), (1, 2, 0, 0, 1), (0, 1, 2, 1),
-    (1, 2, 0, 1, 1), (1, 1, 0, 0), (1, 1, 1, 0), (0, 2, 2, 1, 1), (1, 2, 0, 0, 0), (0, 1, 2, 0), (0, 2, 1, 0, 0),
-    (0, 2, 1, 1, 1), (0, 2, 0, 2, 1), (0, 2, 0, 2, 0), (1, 2, 1, 1, 1), (1, 1, 2, 1), (1, 2, 0, 1, 0),
-    (0, 2, 1, 0, 1), (1, 2, 1, 0, 0), (1, 2, 0, 2, 0), (1, 2, 0, 2, 1), (1, 2, 2, 0, 0), (1, 2, 1, 0, 1),
-    (1, 2, 2, 1, 1), (0, 2, 2, 0, 0), (0, 2, 1, 1, 0), (4, 2), (1, 2, 1, 2, 1), (1, 2, 1, 2, 0), (0, 2, 1, 2, 0),
-    (3, 0, 0), (1, 1, 2, 0), (1, 2, 1, 1, 0), (0, 2, 1, 2, 1), (0, 2, 2, 0, 1), (1, 2, 2, 0, 1), (3, 0, 1),
-    (1, 2, 2, 2, 1), (0, 2, 2, 1, 0), (0, 2, 2, 2, 0), (1, 2, 2, 2, 0), (1, 2, 2, 1, 0), (0, 2, 2, 2, 1),
-    (0, 2, 3, 1, 1), (3, 0, 2), (0, 2, 3, 0, 0), (3, 0, 3), (0, 2, 3, 0, 1), (3, 1, 0), (0, 2, 3, 1, 0),
-    (1, 2, 3, 0, 0), (1, 2, 3, 1, 1), (1, 2, 3, 1, 0), (1, 2, 3, 0, 1), (3, 1, 1), (3, 1, 2), (3, 1, 3), (3, 2, 0),
-    (0, 2, 3, 2, 1), (0, 2, 3, 2, 0), (1, 2, 3, 2, 0), (1, 2, 3, 2, 1), (3, 2, 1), (3, 2, 2), (3, 2, 3), (3, 3, 0),
-    (3, 3, 1), (3, 3, 2), (3, 3, 3),
+    (2, 0), (0, 1, 1, 1), (0, 2, 0, 1, 0), (0, 1, 1, 0), (0, 2, 0, 0, 0), (0, 2, 0, 1, 1), (0, 2, 0, 0, 1),
+    (0, 1, 0, 0), (2, 1), (0, 1, 0, 1), (4, 0), (4, 1), (1, 1, 0, 0), (1, 2, 0, 1, 0), (1, 1, 1, 0), (1, 2, 0, 0, 0),
+    (1, 1, 0, 1), (1, 1, 1, 1), (1, 2, 0, 1, 1), (1, 2, 0, 0, 1), (0, 1, 2, 0), (0, 1, 2, 1), (0, 2, 1, 0, 1),
+    (0, 2, 0, 2, 1), (0, 2, 1, 0, 0), (1, 2, 1, 0, 0), (0, 2, 0, 2, 0), (0, 2, 1, 1, 1), (1, 2, 1, 1, 1),
+    (1, 2, 0, 2, 0), (1, 2, 0, 2, 1), (1, 2, 1, 0, 1), (1, 1, 2, 1), (0, 2, 2, 1, 1), (1, 1, 2, 0), (1, 2, 2, 1, 1),
+    (0, 2, 2, 0, 0), (0, 2, 1, 1, 0), (0, 2, 1, 2, 1), (0, 2, 2, 1, 0), (0, 2, 3, 1, 1), (1, 2, 2, 0, 0), (4, 2),
+    (1, 2, 1, 2, 1), (0, 2, 1, 2, 0), (3, 0, 0), (0, 2, 3, 0, 0), (1, 2, 1, 2, 0), (1, 2, 1, 1, 0), (3, 0, 1),
+    (1, 2, 2, 0, 1), (1, 2, 3, 1, 1), (1, 2, 2, 2, 1), (0, 2, 2, 2, 1), (3, 0, 2), (3, 0, 3), (1, 2, 3, 0, 0),
+    (0, 2, 2, 2, 0), (1, 2, 2, 1, 0), (0, 2, 2, 0, 1), (1, 2, 2, 2, 0), (3, 1, 0), (3, 1, 1), (0, 2, 3, 1, 0),
+    (0, 2, 3, 0, 1), (0, 2, 3, 2, 0), (3, 1, 2), (1, 2, 3, 0, 1), (1, 2, 3, 2, 1), (3, 1, 3), (1, 2, 3, 1, 0),
+    (0, 2, 3, 2, 1), (1, 2, 3, 2, 0), (3, 2, 0), (3, 2, 1), (3, 2, 2), (3, 3, 0), (3, 2, 3), (3, 3, 1), (3, 3, 2),
 )
 
 
@@ -57,7 +56,7 @@
     act, w, s, h1, h2,
     pl_f, pl_g, rc_f, rc_g, ys_f, ry_f,
     fp, gown, sp, st, perm, eye, h1h, h1l, fn, ft,
-    gsb, gb, dg, first_v, second_v,
+    gsb, gb, dg, first_v, second_v, proj,
     gp, rcgp, gs1, r1a, r1b, ab2, r2a, r2b, ab3, r3, fin, dirh, dirf,
     nrm, nrr, nrc,
     local_sem, ga_send, ga_recv, fe_send, fe_recv, gs_send, gs_recv, gg_send, gg_recv,
@@ -253,15 +252,27 @@
     def reduce_f(i):
         fd[i, 4].wait_recv()
         f = ((pl_f[i, c, yl] + rc_f[i, yl]) + ry_f[i]).astype(BF16)
-        fp[:, lanes(chunk_of(0, i))] = f[:, :128]
-        fp[:, lanes(chunk_of(1, i))] = f[:, 128:]
+        total = None
+        for o in (0, 1):
+            p, u, v = part(o)
+            ui = (u + DU[i]) % 4
+            q = p * 4 + ui
+            fo = f[:, 128 * o:128 * o + 128]
+            fp[:, lanes(q)] = fo
+            term = dot(fo, sp[lanes(q), :])
+            total = term if total is None else total + term
+            turned = dot(eye[...], fo, NT).astype(BF16)
+            for j in range(4):
+                at = p * 512 + ui * (128 - 96 * p) + j * (32 + 96 * p)
+                ft[pl.ds(pl.multiple_of(at, 32), 32), :] = turned[j * 32:j * 32 + 32]
+        proj[...] = total if i == 0 else proj[...] + total
 
     def prepare_a():
         n_i = lax.broadcasted_iota(jnp.int32, (512, 512), 0)
         r_i = lax.broadcasted_iota(jnp.int32, (512, 512), 1)
         swapped = ((n_i // 32) % 4) * 128 + (n_i // 128) * 32 + n_i % 32
         perm[...] = (r_i == swapped).astype(F32).astype(BF16)
-        eye[...] = (r_i == n_i).astype(F32).astype(BF16)
+        eye[...] = (r_i == n_i)[:128, :128].astype(F32).astype(BF16)
 
     def prepare_b():
         scopy.wait()
@@ -293,14 +304,13 @@
             elif k < 3:
                 group_f(i, k == 1)
             else:
-                if i < 3:
-                    reduce_core(i)
+                reduce_core(i)
                 if i > 0:
                     reduce_g(i - 1)
-                if i in (1, 2):
                     reduce_f(i - 1)
         else:
             (prepare_a, prepare_b, prepare_c)[op[1]]()
+    reduce_g(2)
     reduce_g(3)
 
     g = gown[...]
@@ -309,16 +319,20 @@
 
     half = width // 2
 
-    def gs_core(ref, k):
-        return send(ref, ref, gs_send.at[k], gs_recv.at[k], core)
-
-    g1 = []
-    for d in (1, 3, 2):
-        a = gsb.at[c, x, z, :, pl.ds(0, half)]
-        b = gsb.at[c, x, z, :, pl.ds(half, half)]
-        g1.append(send(a, a, gs_send.at[d - 1], gs_recv.at[d - 1], xdev(d)))
-        g1.append(send(b, b, gs_send.at[3 + d - 1], gs_recv.at[3 + d - 1], zdev(d)))
-
+    def gs_part(o, bx, bz):
+        return gsb.at[c, bx, bz, :, pl.ds(half * o, half)]
+
+    def gs_go(ref, k, who):
+        return send(ref, ref, gs_send.at[k], gs_recv.at[k], who)
+
+    g1 = {}
+    for d in (1, 3, 2):
+        g1[0, d] = gs_go(gs_part(0, x, z), d - 1, xdev(d))
+        g1[1, d] = gs_go(gs_part(1, x, z), 2 + d, zdev(d))
+    g2 = {}
+    for d in (1, 3, 2):
+        g2[0, 0, d] = gs_go(gs_part(0, x, z), 5 + d, zdev(d))
+        g2[1, 0, d] = gs_go(gs_part(1, x, z), 17 + d, xdev(d))
     reduce_core(3)
 
     at_diag = c * 512 + (x + c * (z - x)) * 128 + (z + c * (x - z)) * 32
@@ -328,16 +342,15 @@
     gb[c, x, z] = jnp.where(on, 0.0, g).astype(BF16)
     dg[c, x, z] = jnp.broadcast_to(jnp.sum(jnp.where(on, g, 0.0), axis=1, keepdims=True), (32, 128))
 
-    wait_all(g1)
-    g2 = []
-    for d in (1, 3, 2):
-        a = gsb.at[c, :, z, :, pl.ds(0, half)]
-        b = gsb.at[c, x, :, :, pl.ds(half, half)]
-        g2.append((d, 0, send(a, a, gs_send.at[6 + d - 1], gs_recv.at[6 + d - 1], zdev(d))))
-        g2.append((d, 1, send(b, b, gs_send.at[9 + d - 1], gs_recv.at[9 + d - 1], xdev(d))))
+    for j in (1, 3, 2):
+        for o in (0, 1):
+            g1[o, j].wait_recv()
+            for d in (1, 3, 2):
+                ref = gs_part(o, (x + 4 - j) % 4, z) if o == 0 else gs_part(o, x, (z + 4 - j) % 4)
+                g2[o, j, d] = gs_go(ref, 5 + 12 * o + 3 * j + d, zdev(d) if o == 0 else xdev(d))
     g3 = [
-        gs_core(gsb.at[c, :, z, :, pl.ds(0, half)], 12),
-        gs_core(gsb.at[c, x, :, :, pl.ds(half, half)], 13),
+        gs_go(gsb.at[c, :, z, :, pl.ds(0, half)], 30, core),
+        gs_go(gsb.at[c, x, :, :, pl.ds(half, half)], 34, core),
     ]
     gg1 = []
     for d in (1, 3, 2):
@@ -348,18 +361,15 @@
         gg1.append(send(b, b, gg_send.at[3 + d - 1], gg_recv.at[3 + d - 1], zdev(d)))
         gg1.append(send(e, e, dg_send.at[d - 1], dg_recv.at[d - 1], xdev(d)))
     reduce_f(2)
-    for d, o, cp in g2:
-        cp.wait_recv()
-        if o == 0:
-            g3.append(gs_core(gsb.at[c, :, (z + 4 - d) % 4, :, pl.ds(0, half)], 14 + d))
-        else:
-            g3.append(gs_core(gsb.at[c, (x + 4 - d) % 4, :, :, pl.ds(half, half)], 17 + d))
-    reduce_f(3)
-    fn[:, :512] = fp[:, :512]
-    fn[:, 512:] = dot(fp[:, 512:], perm[...]).astype(BF16)
-    ft[:512] = dot(eye[...], fp[:, :512], NT).astype(BF16)
-    ft[512:] = dot(perm[...], fp[:, 512:], NT).astype(BF16)
-    proj = dot(fp[...], sp[...])
+    for d in (1, 3, 2):
+        for o in (0, 1):
+            for j in (0, 1, 3, 2):
+                g2[o, j, d].wait_recv()
+            if o == 0:
+                ref = gsb.at[c, :, (z + 4 - d) % 4, :, pl.ds(0, half)]
+            else:
+                ref = gsb.at[c, (x + 4 - d) % 4, :, :, pl.ds(half, half)]
+            g3.append(gs_go(ref, 30 + 4 * o + d, core))
     wait_all(gg1)
     gg2 = []
     for d in (1, 3, 2):
@@ -370,6 +380,7 @@
         gg2.append(send(b, b, gg_send.at[9 + d - 1], gg_recv.at[9 + d - 1], xdev(d)))
         gg2.append(send(e, e, dg_send.at[3 + d - 1], dg_recv.at[3 + d - 1], zdev(d)))
     h2copy.wait()
+    reduce_f(3)
     wait_all(g3)
 
     gs = gsb[...].reshape(1024, width)
@@ -378,23 +389,23 @@
     ip, im = pos_neg(inner)
     h2v = h2[...]
     h2s = split(h2v)
-    num = jnp.maximum(proj, 0.0) + dot3(h2s, im)
-    den = jnp.maximum(-proj, 0.0) + dot3(h2s, ip)
-    second_v[...] = h2v * jnp.sqrt(num / den)
+    pr = proj[...]
+    num = jnp.maximum(pr, 0.0) + dot3(h2s, im)
+    den = jnp.maximum(-pr, 0.0) + dot3(h2s, ip)
+    second = h2v * jnp.sqrt(num / den)
+    second_v[...] = second
     second_copy = pltpu.make_async_copy(second_v, second_hbm, local_sem.at[5])
     second_copy.start()
 
-    def grad_body(j, carry):
-        sn = split(second_v[...])
-        rows = gsb[j // 2, pl.ds((j % 2) * 2, 2)].reshape(256, width)
-        res = dot3(split(rows), sn, NT) - ft[pl.ds(pl.multiple_of(j * 256, 256), 256), :].astype(F32)
+    sn = split(second)
+    k1 = []
+    for p in (0, 1):
+        rows = slice(512 * p, 512 * p + 512)
+        res = dot3((gsh[rows], gsl[rows]), sn, NT) - ft[rows, :].astype(F32)
         gr = dot3(split(res), sn)
-        gp[0, j // 2, pl.ds((j % 2) * 2, 2)] = gr[:, :128].reshape(2, 4, 32, 128)
-        gp[1, j // 2, pl.ds((j % 2) * 2, 2)] = gr[:, 128:].reshape(2, 4, 32, 128)
-        return carry
-
-    lax.fori_loop(0, 4, grad_body, 0)
-    k1 = send(gp.at[1 - c], rcgp, rs_send.at[0], rs_recv.at[0], core)
+        gp[0, p] = gr[:, :128].reshape(4, 4, 32, 128)
+        gp[1, p] = gr[:, 128:].reshape(4, 4, 32, 128)
+        k1.append(send(gp.at[1 - c, p], rcgp.at[p], rs_send.at[17 * p], rs_recv.at[17 * p], core))
 
     def first_body(j, carry):
         gt = gb[j // 2, pl.ds((j % 2) * 2, 2)].reshape(256, 1024)
@@ -408,8 +419,10 @@
         first_v[:, cols] = h * jnp.sqrt(num_ / den_)
         return carry
 
-    k1.wait_recv()
-    gs1[...] = gp[c] + rcgp[...]
+    k1[0].wait_recv()
+    gs1[0] = gp[c, 0] + rcgp[0]
+    k1[1].wait_recv()
+    gs1[1] = gp[c, 1] + rcgp[1]
     k2 = []
     for d in (1, 3, 2):
         k2.append(send(gs1.at[0, (x + d) % 4], r1a.at[d - 1], rs_send.at[d], rs_recv.at[d], xdev(d)))
@@ -423,6 +436,8 @@
     del pending[-8:]
     settle()
     pending.extend(late)
+    fn[:, :512] = fp[:, :512]
+    fn[:, 512:] = dot(fp[:, 512:], perm[...]).astype(BF16)
     wait_all(k2)
     ab2[0] = (gs1[0, x] + r1a[0]) + (r1a[1] + r1a[2])
     ab2[1] = (gs1[1, :, z] + r1b[0]) + (r1b[1] + r1b[2])
@@ -438,9 +453,8 @@
     k4 = []
     for d in (1, 3, 2):
         k4.append(send(ab3, r3.at[d - 1], rs_send.at[12 + d], rs_recv.at[12 + d], ydev(d)))
-    lax.fori_loop(2, 4, first_body, 0)
-    first_copy = pltpu.make_async_copy(first_v, first_hbm, local_sem.at[7])
-    first_copy.start()
+    lax.fori_loop(2, 3, first_body, 0)
+    settle()
     wait_all(k4)
     fin[...] = (ab3[...] + r3[0]) + (r3[1] + r3[2])
 
@@ -454,13 +468,16 @@
                 n1.append(send(nrm.at[0], nrr.at[k], no_send.at[k], no_recv.at[k], plane(dx, dz)))
     dirh[c] = fin[yh]
     k5 = send(dirh.at[c], dirh.at[c], rs_send.at[16], rs_recv.at[16], core)
+    lax.fori_loop(3, 4, first_body, 0)
+    first_copy = pltpu.make_async_copy(first_v, first_hbm, local_sem.at[7])
+    first_copy.start()
     wait_all(n1)
     nrm[1] = nrm[0] + jnp.sum(nrr[...], axis=0)
     n4 = send(nrm.at[1], nrc, no_send.at[15], no_recv.at[15], core)
     settle()
     k5.wait_recv()
     n4.wait_recv()
-    total = jnp.sum(nrm[1] + nrc[...])
+    total = jnp.sum(jnp.sum(nrm[1] + nrc[...], axis=1, keepdims=True), axis=0, keepdims=True)
     scale = jnp.sqrt(total / (1024 * width) + 1e-06)
     dirf[:, :128] = dirh[0] / scale
     dirf[:, 128:] = dirh[1] / scale
@@ -469,6 +486,21 @@
     second_copy.wait()
     first_copy.wait()
     dir_copy.wait()
+
+
+def hand_out(a, b, c, a_out, b_out, c_out, av, bv, cv, sem):
+    loads = [pltpu.make_async_copy(src, held, sem.at[k]) for k, (src, held) in enumerate(((a, av), (b, bv), (c, cv)))]
+    stores = [
+        pltpu.make_async_copy(held, dst, sem.at[3 + k])
+        for k, (held, dst) in enumerate(((av, a_out), (bv, b_out), (cv, c_out)))
+    ]
+    for cp in loads:
+        cp.start()
+    for load, store in zip(loads, stores):
+        load.wait()
+        store.start()
+    for cp in stores:
+        cp.wait()
 
 
 def shards(activations, dictionary, second_factor, first_codes, second_codes):
@@ -482,17 +514,17 @@
         v((4, 2, sub, 256), F32), v((4, 3, 32, 256), F32),
         v((4, sub, 256), F32), v((4, sub, 256), F32),
         v((sub, k1), BF16), v((32, k1), F32), v((k1, k2), BF16), v((k2, k1), BF16),
-        v((512, 512), BF16), v((512, 512), BF16), v((sub, k1), BF16), v((sub, k1), BF16),
+        v((512, 512), BF16), v((128, 128), BF16), v((sub, k1), BF16), v((sub, k1), BF16),
         v((sub, k1), BF16), v((k1, sub), BF16),
         v((2, 4, 4, 32, k2), F32), v((2, 4, 4, 32, k1), BF16), v((2, 4, 4, 32, 128), F32),
-        v((sub, k1), F32), v((sub, k2), F32),
+        v((sub, k1), F32), v((sub, k2), F32), v((sub, k2), F32),
         v((2, 2, 4, 4, 32, 128), F32), v((2, 4, 4, 32, 128), F32), v((2, 4, 4, 32, 128), F32),
         v((3, 4, 32, 128), F32), v((3, 4, 32, 128), F32), v((2, 4, 32, 128), F32),
         v((3, 32, 128), F32), v((3, 32, 128), F32), v((2, 32, 128), F32), v((3, 2, 32, 128), F32),
         v((2, 32, 128), F32), v((2, 32, 128), F32), v((32, 256), F32),
         v((2, 8, 128), F32), v((15, 8, 128), F32), v((8, 128), F32),
-        dma((8,)), dma((3, 30)), dma((3, 30)), dma((4, 5)), dma((4, 5)), dma((21,)), dma((21,)), dma((13,)), dma((13,)),
-        dma((7,)), dma((7,)), dma((17,)), dma((17,)), dma((16,)), dma((16,)),
+        dma((8,)), dma((3, 30)), dma((3, 30)), dma((4, 5)), dma((4, 5)), dma((38,)), dma((38,)), dma((13,)), dma((13,)),
+        dma((7,)), dma((7,)), dma((18,)), dma((18,)), dma((16,)), dma((16,)),
     ]
     hbm = pl.BlockSpec(memory_space=pl.ANY)
     first, second, direction = pl.pallas_call(
@@ -510,6 +542,14 @@
         ),
         name="sweep",
     )(activations.reshape(2, 2, sub, rows), dictionary.T, second_factor, first_codes.reshape(sub, k1), second_codes.reshape(sub, k2))
+    first, second, direction = pl.pallas_call(
+        hand_out,
+        out_shape=tuple(jax.ShapeDtypeStruct(o.shape, F32) for o in (first, second, direction)),
+        in_specs=[hbm] * 3,
+        out_specs=(hbm,) * 3,
+        scratch_shapes=[v((sub, k1), F32), v((sub, k2), F32), v((32, k2), F32), dma((6,))],
+        name="hand_out",
+    )(first, second, direction)
     return first.reshape(first_codes.shape), second.reshape(second_codes.shape), direction
 
 

time: 107 us -> 98.2 us (0.918)
  local copies, waits for them, and re-layouts: 5.35 us -> 0 us
  Pallas kernels: 100 us -> 97.2 us
    pallas_call x1, Pallas kernels: 100 us -> 94.9 us  [shards(): pl.pallas_call(kernel, out_shape=(jax.ShapeDtypeStruct((sub, k1), F32), j...]
    unnamed x3 -> x0, local copies, waits for them, and re-layouts: 5.35 us -> none
    pallas_call x0 -> x1, Pallas kernels: none -> 2.33 us  [shards(): pl.pallas_call(hand_out, out_shape=tuple((jax.ShapeDtypeStruct(o.shape, F...]
where the time goes in v3:
time: 98.2 us; the launch traced here: 98 us
  Pallas kernels  97.2 us (99%)
    pallas_call x1, Pallas kernels, shards(): pl.pallas_call(kernel, out_shape=(jax.ShapeDtypeStruct((sub, k1), F32), j...  94.9 us
    pallas_call x1, Pallas kernels, shards(): pl.pallas_call(hand_out, out_shape=tuple((jax.ShapeDtypeStruct(o.shape, F...  2.33 us

profile of v3, /device:TPU:1, one launch (start us, length us, event | category | flops | bytes accessed | tf_op | source)
XLA Modules:
  0.0 98.0 jit_solution(8070726719249346552)
XLA Ops:
  0.6 94.9 %sweep.1 = (f32[256,1024]{1,0:T(8,128)}, f32[256,256]{1,0:T(8,128)}, f32[32,256]{1,0:T(8,128)}) custom-call(bf16[2,2,256,3584]{3,2,1,0:T(8,128)(2,1)} %bitcast.6, bf16[32,3584]{1,0:T(8,128)(2,1)} %bitcast.9, bf16[1024,256]{1,0:T(8,128)(2,1)} %s_hbm.1, f32[256,1024]{1,0:T(8,128)} %bitcast.7, f32[256,256]{1,0:T(8,128)} %bitcast.8), custom_call_target="tpu_custom_call" | custom-call | tf_op jit(solution)/shard_map/sweep/pallas_call | solution.py:530
  95.5 2.3 %hand_out.1 = (f32[256,1024]{1,0:T(8,128)}, f32[256,256]{1,0:T(8,128)}, f32[32,256]{1,0:T(8,128)}) custom-call(f32[256,1024]{1,0:T(8,128)} %get-tuple-element.9.a, f32[256,256]{1,0:T(8,128)} %get-tuple-element.10.b, f32[32,256]{1,0:T(8,128)} %get-tuple-element.11.c), custom_call_target="tpu_custom_call" | custom-call | tf_op jit(solution)/shard_map/hand_out/pallas_call | solution.py:545

commit v4 on v3

--- a/solution.py
+++ b/solution.py
@@ -36,17 +36,18 @@
 
 
 ORDER = (
-    (2, 0), (0, 1, 1, 1), (0, 2, 0, 1, 0), (0, 1, 1, 0), (0, 2, 0, 0, 0), (0, 2, 0, 1, 1), (0, 2, 0, 0, 1),
-    (0, 1, 0, 0), (2, 1), (0, 1, 0, 1), (4, 0), (4, 1), (1, 1, 0, 0), (1, 2, 0, 1, 0), (1, 1, 1, 0), (1, 2, 0, 0, 0),
-    (1, 1, 0, 1), (1, 1, 1, 1), (1, 2, 0, 1, 1), (1, 2, 0, 0, 1), (0, 1, 2, 0), (0, 1, 2, 1), (0, 2, 1, 0, 1),
-    (0, 2, 0, 2, 1), (0, 2, 1, 0, 0), (1, 2, 1, 0, 0), (0, 2, 0, 2, 0), (0, 2, 1, 1, 1), (1, 2, 1, 1, 1),
-    (1, 2, 0, 2, 0), (1, 2, 0, 2, 1), (1, 2, 1, 0, 1), (1, 1, 2, 1), (0, 2, 2, 1, 1), (1, 1, 2, 0), (1, 2, 2, 1, 1),
-    (0, 2, 2, 0, 0), (0, 2, 1, 1, 0), (0, 2, 1, 2, 1), (0, 2, 2, 1, 0), (0, 2, 3, 1, 1), (1, 2, 2, 0, 0), (4, 2),
-    (1, 2, 1, 2, 1), (0, 2, 1, 2, 0), (3, 0, 0), (0, 2, 3, 0, 0), (1, 2, 1, 2, 0), (1, 2, 1, 1, 0), (3, 0, 1),
-    (1, 2, 2, 0, 1), (1, 2, 3, 1, 1), (1, 2, 2, 2, 1), (0, 2, 2, 2, 1), (3, 0, 2), (3, 0, 3), (1, 2, 3, 0, 0),
-    (0, 2, 2, 2, 0), (1, 2, 2, 1, 0), (0, 2, 2, 0, 1), (1, 2, 2, 2, 0), (3, 1, 0), (3, 1, 1), (0, 2, 3, 1, 0),
-    (0, 2, 3, 0, 1), (0, 2, 3, 2, 0), (3, 1, 2), (1, 2, 3, 0, 1), (1, 2, 3, 2, 1), (3, 1, 3), (1, 2, 3, 1, 0),
-    (0, 2, 3, 2, 1), (1, 2, 3, 2, 0), (3, 2, 0), (3, 2, 1), (3, 2, 2), (3, 3, 0), (3, 2, 3), (3, 3, 1), (3, 3, 2),
+    (2, 0), (0, 2, 0, 1, 1), (0, 1, 1, 1), (0, 2, 0, 0, 0), (0, 1, 1, 0), (0, 2, 0, 1, 0), (0, 1, 0, 0),
+    (0, 2, 0, 0, 1), (0, 1, 0, 1), (2, 1), (4, 0), (4, 1), (1, 1, 1, 0), (1, 2, 0, 0, 0), (0, 1, 2, 1), (1, 1, 0, 0),
+    (1, 1, 0, 1), (0, 2, 0, 2, 1), (1, 2, 0, 0, 1), (1, 2, 0, 1, 0), (0, 1, 2, 0), (1, 1, 1, 1), (1, 2, 0, 1, 1),
+    (0, 2, 0, 2, 0), (0, 2, 1, 0, 0), (0, 2, 2, 1, 1), (1, 1, 2, 0), (1, 2, 0, 2, 0), (1, 2, 1, 1, 0),
+    (1, 2, 1, 0, 0), (1, 2, 2, 0, 0), (0, 2, 2, 0, 0), (1, 2, 1, 1, 1), (0, 2, 1, 1, 1), (1, 2, 0, 2, 1),
+    (1, 1, 2, 1), (0, 2, 1, 1, 0), (1, 2, 2, 1, 1), (0, 2, 1, 2, 0), (1, 2, 1, 0, 1), (0, 2, 1, 2, 1),
+    (0, 2, 2, 1, 0), (1, 2, 1, 2, 0), (1, 2, 3, 0, 0), (0, 2, 3, 1, 1), (0, 2, 1, 0, 1), (4, 2), (1, 2, 1, 2, 1),
+    (0, 2, 3, 0, 0), (3, 0, 0), (1, 2, 2, 1, 0), (3, 0, 1), (0, 2, 2, 0, 1), (1, 2, 2, 0, 1), (0, 2, 2, 2, 1),
+    (1, 2, 3, 1, 1), (1, 2, 2, 2, 1), (0, 2, 2, 2, 0), (3, 0, 2), (3, 0, 3), (1, 2, 2, 2, 0), (0, 2, 3, 1, 0),
+    (3, 1, 0), (0, 2, 3, 0, 1), (1, 2, 3, 0, 1), (1, 2, 3, 1, 0), (3, 1, 1), (3, 1, 2), (0, 2, 3, 2, 1),
+    (1, 2, 3, 2, 0), (1, 2, 3, 2, 1), (0, 2, 3, 2, 0), (3, 1, 3), (3, 2, 0), (3, 2, 1), (3, 2, 2), (3, 0, 4), (3, 3, 0),
+    (3, 2, 3), (3, 3, 1),
 )
 
 
@@ -54,11 +55,11 @@
     act_hbm, dt_hbm, s_hbm, h1_hbm, h2_hbm,
     first_hbm, second_hbm, dir_hbm,
     act, w, s, h1, h2,
-    pl_f, pl_g, rc_f, rc_g, ys_f, ry_f,
+    pl_f, pl_g, rc_f, rc_g, ys_f, ys_g, ry_f,
     fp, gown, sp, st, perm, eye, h1h, h1l, fn, ft,
     gsb, gb, dg, first_v, second_v, proj,
     gp, rcgp, gs1, r1a, r1b, ab2, r2a, r2b, ab3, r3, fin, dirh, dirf,
-    nrm, nrr, nrc,
+    nrm, nrr,
     local_sem, ga_send, ga_recv, fe_send, fe_recv, gs_send, gs_recv, gg_send, gg_recv,
     dg_send, dg_recv, rs_send, rs_recv, no_send, no_recv,
 ):
@@ -104,8 +105,7 @@
     acopy.start()
 
     barrier = pltpu.get_barrier_semaphore()
-    peers = [plane(dx, dz) for dx in range(4) for dz in range(4) if dx + dz > 0]
-    peers += [ydev(1), ydev(2), ydev(3), core, ylc]
+    peers = [xdev(1), xdev(3), zdev(1), zdev(3), ydev(1), ydev(2), ydev(3), core, ylc]
     for who in peers:
         pl.semaphore_signal(barrier, inc=1, device_id=who, device_id_type=MESH)
     pl.semaphore_wait(barrier, len(peers))
@@ -224,6 +224,8 @@
         g = dot(lrows, weights(i), NT)
         pl_g[i] = g.reshape(2, 32, g.shape[1])
         fd[i, 0] = send(pl_g.at[i, 1 - c], rc_g.at[i, 0], fe_send.at[i, 0], fe_recv.at[i, 0], core)
+        if i < 3:
+            return
         fd[i, 1] = send(pl_g.at[i, c], rc_g.at[i, 1], fe_send.at[i, 1], fe_recv.at[i, 1], ylp)
         fd[i, 2] = send(pl_g.at[i, 1 - c], rc_g.at[i, 2], fe_send.at[i, 2], fe_recv.at[i, 2], ylc)
 
@@ -235,23 +237,33 @@
             fd[i, 3] = send(pl_f.at[i, cc], rc_f.at[i], fe_send.at[i, 3], fe_recv.at[i, 3], core)
 
     def reduce_core(i):
+        if i < 3:
+            fd[i, 0].wait_recv()
+            ys_g[i] = pl_g[i, c] + rc_g[i, 0]
+            fd[i, 1] = send(ys_g.at[i], rc_g.at[i, 1], fe_send.at[i, 1], fe_recv.at[i, 1], ylp)
         fd[i, 3].wait_recv()
-        ys_f[i] = pl_f[i, c, 1 - yl] + rc_f[i, 1 - yl]
-        fd[i, 4] = send(ys_f.at[i], ry_f.at[i], fe_send.at[i, 4], fe_recv.at[i, 4], ylp)
+        out, back = (ys_f.at[i], ry_f.at[i])
+        out[...] = (pl_f[i, c, 1 - yl] + rc_f[i, 1 - yl]).astype(out.dtype)
+        fd[i, 4] = send(out, back, fe_send.at[i, 4], fe_recv.at[i, 4], ylp)
 
     def lanes(q):
         return pl.ds(pl.multiple_of(q * 128, 128), 128)
 
     def reduce_g(i):
-        for k in range(3):
-            fd[i, k].wait_recv()
-        g = (pl_g[i, c] + rc_g[i, 0]) + (rc_g[i, 1] + rc_g[i, 2])
+        if i < 3:
+            fd[i, 1].wait_recv()
+            g = ys_g[i] + rc_g[i, 1]
+        else:
+            for k in range(3):
+                fd[i, k].wait_recv()
+            g = (pl_g[i, c] + rc_g[i, 0]) + (rc_g[i, 1] + rc_g[i, 2])
         gown[:, lanes(chunk_of(0, i))] = g[:, :128]
         gown[:, lanes(chunk_of(1, i))] = g[:, 128:]
 
     def reduce_f(i):
         fd[i, 4].wait_recv()
-        f = ((pl_f[i, c, yl] + rc_f[i, yl]) + ry_f[i]).astype(BF16)
+        back = ry_f[i]
+        f = ((pl_f[i, c, yl] + rc_f[i, yl]) + back).astype(BF16)
         total = None
         for o in (0, 1):
             p, u, v = part(o)
@@ -303,11 +315,12 @@
                 group_g(i)
             elif k < 3:
                 group_f(i, k == 1)
+            elif k == 4:
+                reduce_f(i)
             else:
                 reduce_core(i)
                 if i > 0:
                     reduce_g(i - 1)
-                    reduce_f(i - 1)
         else:
             (prepare_a, prepare_b, prepare_c)[op[1]]()
     reduce_g(2)
@@ -333,12 +346,14 @@
     for d in (1, 3, 2):
         g2[0, 0, d] = gs_go(gs_part(0, x, z), 5 + d, zdev(d))
         g2[1, 0, d] = gs_go(gs_part(1, x, z), 17 + d, xdev(d))
+    group_f(3, False)
     reduce_core(3)
 
     at_diag = c * 512 + (x + c * (z - x)) * 128 + (z + c * (x - z)) * 32
     lane = lax.broadcasted_iota(jnp.int32, g.shape, 1)
     row = lax.broadcasted_iota(jnp.int32, g.shape, 0)
     on = lane == at_diag + row
+    reduce_f(1)
     gb[c, x, z] = jnp.where(on, 0.0, g).astype(BF16)
     dg[c, x, z] = jnp.broadcast_to(jnp.sum(jnp.where(on, g, 0.0), axis=1, keepdims=True), (32, 128))
 
@@ -360,7 +375,15 @@
         gg1.append(send(a, a, gg_send.at[d - 1], gg_recv.at[d - 1], xdev(d)))
         gg1.append(send(b, b, gg_send.at[3 + d - 1], gg_recv.at[3 + d - 1], zdev(d)))
         gg1.append(send(e, e, dg_send.at[d - 1], dg_recv.at[d - 1], xdev(d)))
-    reduce_f(2)
+    wait_all(gg1)
+    gg2 = []
+    for d in (1, 3, 2):
+        a = gb.at[c, :, z, :, pl.ds(0, 512)]
+        b = gb.at[c, x, :, :, pl.ds(512, 512)]
+        e = dg.at[c, :, z]
+        gg2.append(send(a, a, gg_send.at[6 + d - 1], gg_recv.at[6 + d - 1], zdev(d)))
+        gg2.append(send(b, b, gg_send.at[9 + d - 1], gg_recv.at[9 + d - 1], xdev(d)))
+        gg2.append(send(e, e, dg_send.at[3 + d - 1], dg_recv.at[3 + d - 1], zdev(d)))
     for d in (1, 3, 2):
         for o in (0, 1):
             for j in (0, 1, 3, 2):
@@ -370,15 +393,7 @@
             else:
                 ref = gsb.at[c, (x + 4 - d) % 4, :, :, pl.ds(half, half)]
             g3.append(gs_go(ref, 30 + 4 * o + d, core))
-    wait_all(gg1)
-    gg2 = []
-    for d in (1, 3, 2):
-        a = gb.at[c, :, z, :, pl.ds(0, 512)]
-        b = gb.at[c, x, :, :, pl.ds(512, 512)]
-        e = dg.at[c, :, z]
-        gg2.append(send(a, a, gg_send.at[6 + d - 1], gg_recv.at[6 + d - 1], zdev(d)))
-        gg2.append(send(b, b, gg_send.at[9 + d - 1], gg_recv.at[9 + d - 1], xdev(d)))
-        gg2.append(send(e, e, dg_send.at[3 + d - 1], dg_recv.at[3 + d - 1], zdev(d)))
+    reduce_f(2)
     h2copy.wait()
     reduce_f(3)
     wait_all(g3)
@@ -419,13 +434,14 @@
         first_v[:, cols] = h * jnp.sqrt(num_ / den_)
         return carry
 
+    k2 = []
     k1[0].wait_recv()
     gs1[0] = gp[c, 0] + rcgp[0]
+    for d in (1, 3, 2):
+        k2.append(send(gs1.at[0, (x + d) % 4], r1a.at[d - 1], rs_send.at[d], rs_recv.at[d], xdev(d)))
     k1[1].wait_recv()
     gs1[1] = gp[c, 1] + rcgp[1]
-    k2 = []
-    for d in (1, 3, 2):
-        k2.append(send(gs1.at[0, (x + d) % 4], r1a.at[d - 1], rs_send.at[d], rs_recv.at[d], xdev(d)))
+    for d in (1, 3, 2):
         k2.append(send(gs1.at[1, :, (z + d) % 4], r1b.at[d - 1], rs_send.at[3 + d], rs_recv.at[3 + d], zdev(d)))
     wait_all(gg2)
     gg3 = [
@@ -459,25 +475,22 @@
     fin[...] = (ab3[...] + r3[0]) + (r3[1] + r3[2])
 
     sq = fin[0] * fin[0] + fin[1] * fin[1]
-    nrm[0] = (sq[0:8] + sq[8:16]) + (sq[16:24] + sq[24:32])
+    nrm[...] = (sq[0:8] + sq[8:16]) + (sq[16:24] + sq[24:32])
     n1 = []
-    for dx in range(4):
-        for dz in range(4):
-            k = dx * 4 + dz - 1
-            if k >= 0:
-                n1.append(send(nrm.at[0], nrr.at[k], no_send.at[k], no_recv.at[k], plane(dx, dz)))
+    for k in range(31):
+        dc, dx, dz = (k + 1) // 16, (k + 1) // 4 % 4, (k + 1) % 4
+        who = dev(yl, (c + dc) % 2, yh, (x + dx) % 4, (z + dz) % 4)
+        n1.append(send(nrm, nrr.at[k], no_send.at[k], no_recv.at[k], who))
     dirh[c] = fin[yh]
     k5 = send(dirh.at[c], dirh.at[c], rs_send.at[16], rs_recv.at[16], core)
     lax.fori_loop(3, 4, first_body, 0)
     first_copy = pltpu.make_async_copy(first_v, first_hbm, local_sem.at[7])
     first_copy.start()
     wait_all(n1)
-    nrm[1] = nrm[0] + jnp.sum(nrr[...], axis=0)
-    n4 = send(nrm.at[1], nrc, no_send.at[15], no_recv.at[15], core)
     settle()
     k5.wait_recv()
-    n4.wait_recv()
-    total = jnp.sum(jnp.sum(nrm[1] + nrc[...], axis=1, keepdims=True), axis=0, keepdims=True)
+    tiles = nrm[...] + jnp.sum(nrr[...], axis=0)
+    total = jnp.sum(jnp.sum(tiles, axis=1, keepdims=True), axis=0, keepdims=True)
     scale = jnp.sqrt(total / (1024 * width) + 1e-06)
     dirf[:, :128] = dirh[0] / scale
     dirf[:, 128:] = dirh[1] / scale
@@ -512,7 +525,7 @@
         v((2, 2, sub, rows), BF16), v((32, 32, rows), BF16), v((k1, k2), BF16), v((sub, k1), F32), v((sub, k2), F32),
         v((4, 2, 2, sub, 256), F32), v((4, 2, 32, 256), F32),
         v((4, 2, sub, 256), F32), v((4, 3, 32, 256), F32),
-        v((4, sub, 256), F32), v((4, sub, 256), F32),
+        v((4, sub, 256), F32), v((3, 32, 256), F32), v((4, sub, 256), F32),
         v((sub, k1), BF16), v((32, k1), F32), v((k1, k2), BF16), v((k2, k1), BF16),
         v((512, 512), BF16), v((128, 128), BF16), v((sub, k1), BF16), v((sub, k1), BF16),
         v((sub, k1), BF16), v((k1, sub), BF16),
@@ -522,9 +535,9 @@
         v((3, 4, 32, 128), F32), v((3, 4, 32, 128), F32), v((2, 4, 32, 128), F32),
         v((3, 32, 128), F32), v((3, 32, 128), F32), v((2, 32, 128), F32), v((3, 2, 32, 128), F32),
         v((2, 32, 128), F32), v((2, 32, 128), F32), v((32, 256), F32),
-        v((2, 8, 128), F32), v((15, 8, 128), F32), v((8, 128), F32),
+        v((8, 128), F32), v((31, 8, 128), F32),
         dma((8,)), dma((3, 30)), dma((3, 30)), dma((4, 5)), dma((4, 5)), dma((38,)), dma((38,)), dma((13,)), dma((13,)),
-        dma((7,)), dma((7,)), dma((18,)), dma((18,)), dma((16,)), dma((16,)),
+        dma((7,)), dma((7,)), dma((18,)), dma((18,)), dma((31,)), dma((31,)),
     ]
     hbm = pl.BlockSpec(memory_space=pl.ANY)
     first, second, direction = pl.pallas_call(

time: 98.2 us -> 96.5 us (0.983)
  Pallas kernels: 97.2 us -> 95.6 us
    pallas_call x1, Pallas kernels: 94.9 us -> 93.2 us  [shards(): pl.pallas_call(kernel, out_shape=(jax.ShapeDtypeStruct((sub, k1), F32), j...]
where the time goes in v4:
time: 96.5 us; the launch traced here: 96.4 us
  Pallas kernels  95.6 us (99%)
    pallas_call x1, Pallas kernels, shards(): pl.pallas_call(kernel, out_shape=(jax.ShapeDtypeStruct((sub, k1), F32), j...  93.2 us
    pallas_call x1, Pallas kernels, shards(): pl.pallas_call(hand_out, out_shape=tuple((jax.ShapeDtypeStruct(o.shape, F...  2.33 us

profile of v4, /device:TPU:1, one launch (start us, length us, event | category | flops | bytes accessed | tf_op | source)
XLA Modules:
  0.0 96.4 jit_solution(15512784232569596929)
XLA Ops:
  0.6 93.2 %sweep.1 = (f32[256,1024]{1,0:T(8,128)}, f32[256,256]{1,0:T(8,128)}, f32[32,256]{1,0:T(8,128)}) custom-call(bf16[2,2,256,3584]{3,2,1,0:T(8,128)(2,1)} %bitcast.6, bf16[32,3584]{1,0:T(8,128)(2,1)} %bitcast.9, bf16[1024,256]{1,0:T(8,128)(2,1)} %s_hbm.1, f32[256,1024]{1,0:T(8,128)} %bitcast.7, f32[256,256]{1,0:T(8,128)} %bitcast.8), custom_call_target="tpu_custom_call" | custom-call | tf_op jit(solution)/shard_map/sweep/pallas_call | solution.py:543
  93.9 2.3 %hand_out.1 = (f32[256,1024]{1,0:T(8,128)}, f32[256,256]{1,0:T(8,128)}, f32[32,256]{1,0:T(8,128)}) custom-call(f32[256,1024]{1,0:T(8,128)} %get-tuple-element.9.a, f32[256,256]{1,0:T(8,128)} %get-tuple-element.10.b, f32[32,256]{1,0:T(8,128)} %get-tuple-element.11.c), custom_call_target="tpu_custom_call" | custom-call | tf_op jit(solution)/shard_map/hand_out/pallas_call | solution.py:558

commit v5 on v4

--- a/solution.py
+++ b/solution.py
@@ -487,7 +487,6 @@
     first_copy = pltpu.make_async_copy(first_v, first_hbm, local_sem.at[7])
     first_copy.start()
     wait_all(n1)
-    settle()
     k5.wait_recv()
     tiles = nrm[...] + jnp.sum(nrr[...], axis=0)
     total = jnp.sum(jnp.sum(tiles, axis=1, keepdims=True), axis=0, keepdims=True)
@@ -496,6 +495,7 @@
     dirf[:, 128:] = dirh[1] / scale
     dir_copy = pltpu.make_async_copy(dirf, dir_hbm, local_sem.at[6])
     dir_copy.start()
+    settle()
     second_copy.wait()
     first_copy.wait()
     dir_copy.wait()

time: 96.5 us -> 96.4 us (level)
  no operation moved by 1% of the time
where the time goes in v5:
time: 96.4 us; the launch traced here: 96.3 us
  Pallas kernels  95.5 us (99%)
    pallas_call x1, Pallas kernels, shards(): pl.pallas_call(kernel, out_shape=(jax.ShapeDtypeStruct((sub, k1), F32), j...  93.2 us
    pallas_call x1, Pallas kernels, shards(): pl.pallas_call(hand_out, out_shape=tuple((jax.ShapeDtypeStruct(o.shape, F...  2.33 us

profile of v5, /device:TPU:1, one launch (start us, length us, event | category | flops | bytes accessed | tf_op | source)
XLA Modules:
  0.0 96.3 jit_solution(315006931485836398)
XLA Ops:
  0.6 93.2 %sweep.1 = (f32[256,1024]{1,0:T(8,128)}, f32[256,256]{1,0:T(8,128)}, f32[32,256]{1,0:T(8,128)}) custom-call(bf16[2,2,256,3584]{3,2,1,0:T(8,128)(2,1)} %bitcast.6, bf16[32,3584]{1,0:T(8,128)(2,1)} %bitcast.9, bf16[1024,256]{1,0:T(8,128)(2,1)} %s_hbm.1, f32[256,1024]{1,0:T(8,128)} %bitcast.7, f32[256,256]{1,0:T(8,128)} %bitcast.8), custom_call_target="tpu_custom_call" | custom-call | tf_op jit(solution)/shard_map/sweep/pallas_call | solution.py:543
  93.8 2.3 %hand_out.1 = (f32[256,1024]{1,0:T(8,128)}, f32[256,256]{1,0:T(8,128)}, f32[32,256]{1,0:T(8,128)}) custom-call(f32[256,1024]{1,0:T(8,128)} %get-tuple-element.9.a, f32[256,256]{1,0:T(8,128)} %get-tuple-element.10.b, f32[32,256]{1,0:T(8,128)} %get-tuple-element.11.c), custom_call_target="tpu_custom_call" | custom-call | tf_op jit(solution)/shard_map/hand_out/pallas_call | solution.py:558
